TPU v7x, 256 devices: a whole 4x4x8 slice. The times are simulated.
256 devices in a mesh: col: 64 (over z_hi, y, x, core), row: 4 (over z_lo).
Axes of the slice: x: 4, y: 4, z: 8 (z_hi: 2, z_lo: 4; z = z_hi * 4 + z_lo), core: 2. Of those that a mesh axis runs over, the one named last changes fastest.
Arguments:
- greens_matrix: float32 [16384, 16384], P('col', 'row'), may hold values from -6 to 6
- dest_ids: int32 [16384], P('col'), may hold values from 0 to 16383, as said below
- send_slot: int32 [64], P('col'), may hold values from 0 to 1
Outputs:
- rotated: float32 [16384, 16384], P('col', 'row')
Inputs may be any that keep to these rules, and one draw needn't show every extreme that they name: `dest_ids`: every value occurs once. Value v belongs to the device v // 256 of col. The sources that one device holds go to at most 8 of any one device's values, and every device sends exactly 8 to one device and receives exactly 8 from one device. The number that device s sends to device (s + o) mod 64 depends on o only.
All inputs are finite; a program needn't handle non-finite values.
Results may differ from a plain program's by a relative error of at most 0.00055.
Values sent between devices are 32-bit elements; how exact they have to be, the bound alone decides.
A program may use at most 128 MiB of HBM per device.

v0:
```python
import jax
import jax.numpy as jnp
from jax import lax
from jax.sharding import PartitionSpec as P

SWEEPS = 2


def from_partner(array, axis, distance):
    return lax.ppermute(array, axis, [(i, i ^ 1 << distance) for i in range(lax.axis_size(axis))])


def orthogonal_steps(pair_gram):
    size = pair_gram.shape[0]
    rotation = jnp.eye(size, dtype=jnp.float32)
    for sweep_index in range(SWEEPS):
        squared = jnp.dot(pair_gram, pair_gram, precision=lax.Precision.HIGHEST)
        factor = jnp.linalg.cholesky(squared)
        q_transposed = jax.scipy.linalg.solve_triangular(factor, pair_gram, lower=True)
        left_side = jnp.dot(q_transposed, pair_gram, precision=lax.Precision.HIGHEST)
        rotated_gram = jnp.dot(left_side, q_transposed.T, precision=lax.Precision.HIGHEST)
        pair_gram = 0.5 * (rotated_gram + rotated_gram.T)
        rotation = jnp.dot(rotation, q_transposed.T, precision=lax.Precision.HIGHEST)
    return (rotation, pair_gram)


def body(greens_matrix, dest_ids, send_slot):
    pair_cols = greens_matrix.shape[0]
    half_cols = pair_cols // 2
    row_count = greens_matrix.shape[1]
    peer_count = lax.axis_size("col")
    cap_slots = max(2, 2 * pair_cols // peer_count)
    slot_count = peer_count * cap_slots
    local_iota = jnp.arange(pair_cols, dtype=jnp.int32)
    target_dev = dest_ids // pair_cols
    target_pos = dest_ids % pair_cols
    same_target = target_dev[:, None] == target_dev[None, :]
    earlier = local_iota[None, :] < local_iota[:, None]
    rank_local = jnp.sum((same_target & earlier).astype(jnp.int32), axis=1)
    slot_local = target_dev * cap_slots + rank_local
    source_of_slot = jnp.full((slot_count,), pair_cols, jnp.int32).at[slot_local].set(local_iota)
    padded = jnp.concatenate([greens_matrix, jnp.zeros((1, row_count), jnp.float32)], axis=0)
    outgoing = padded[source_of_slot]
    position_of_slot = jnp.full((slot_count,), pair_cols, jnp.int32).at[slot_local].set(target_pos)
    arrived, arrived_pos = (
        lax.all_to_all(outgoing, "col", split_axis=0, concat_axis=0, tiled=True),
        lax.all_to_all(position_of_slot, "col", split_axis=0, concat_axis=0, tiled=True),
    )
    slot_iota = jnp.arange(slot_count, dtype=jnp.int32)
    slot_of_position = (
        jnp.zeros((pair_cols,), jnp.int32).at[arrived_pos].set(slot_iota, mode="drop")
    )
    placed = arrived[slot_of_position]
    partial_value = jnp.dot(placed, placed.T, precision=lax.Precision.HIGHEST)
    pair_gram = lax.psum(partial_value, "row")
    rotation, rotated_gram = orthogonal_steps(pair_gram)
    turned = jnp.dot(rotation.T, placed, precision=lax.Precision.HIGHEST)
    send_first = send_slot[0] == 0
    outbound = jnp.where(send_first, turned[:half_cols], turned[half_cols:])
    retained = jnp.where(send_first, turned[half_cols:], turned[:half_cols])
    swap_bit = peer_count.bit_length() - 2
    received = from_partner(outbound, "col", swap_bit)
    paired = jnp.concatenate([retained, received], axis=0)
    second_partial = jnp.dot(paired, paired.T, precision=lax.Precision.HIGHEST)
    second_gram = lax.psum(second_partial, "row")
    final_rotation, final_gram = orthogonal_steps(second_gram)
    return jnp.dot(final_rotation.T, paired, precision=lax.Precision.HIGHEST)


def solution(mesh):
    return jax.shard_map(
        body,
        mesh=mesh,
        in_specs=(P("col", "row"), P("col"), P("col")),
        out_specs=P("col", "row"),
        check_vma=False,
    )
```

profile of v0, /device:TPU:1, one launch (start us, length us, event | category | flops | bytes accessed | tf_op | source)
XLA Modules:
  0.0 737.2 jit_solution(4164846366144902838)
XLA Ops:
  6.5 0.7 and_select_fusion
  7.4 1.4 scatter_custom_fusion.1
  8.8 0.7 all_to_all.19
  9.5 15.6 %all-to-all-start.1 = ((s32[64,8,1]{1,2,0:T(1,128)}), s32[64,8,1]{1,2,0:T(1,128)S(1)}, u32[]{:S(2)}, u32[]{:S(2)}) async-start(s32[64,8,1]{1,2,0:T(1,128)} %bitcast.3), calls=%async_computation.1 | async-start | bytes 65536 | tf_op jit(solution)/shard_map/all_to_all | solution.py:47
  25.2 1.4 scatter_custom_fusion
  26.6 4.8 concatenate.8
  31.4 11.1 %gather_fusion = f32[512,4096]{1,0:T(8,128)} fusion(f32[257,4096]{1,0:T(8,128)} %concatenate.8, s32[1024]{0:T(1024)S(1)} %pad_clamp_fusion.1), kind=kCustom, calls=%fused_computation | custom fusion | bytes 16779264 | tf_op jit(solution)/shard_map/gather | solution.py:43
  42.4 13.0 %all-to-all-start = ((f32[64,8,4096]{2,1,0:T(8,128)}), f32[64,8,4096]{2,1,0:T(8,128)}, u32[]{:S(2)}, u32[]{:S(2)}) async-start(f32[64,8,4096]{2,1,0:T(8,128)} %bitcast.156), calls=%async_computation | async-start | bytes 16777216 | tf_op jit(solution)/shard_map/all_to_all | solution.py:46
  56.0 0.7 reduce.11
  56.8 2.6 scatter_custom_fusion.2
  59.5 181.7 %all-to-all-done = f32[64,8,4096]{2,1,0:T(8,128)} async-done(((f32[64,8,4096]{2,1,0:T(8,128)}), f32[64,8,4096]{2,1,0:T(8,128)}, u32[]{:S(2)}, u32[]{:S(2)}) %all-to-all-start) | async-done | bytes 8388640 | tf_op jit(solution)/shard_map/all_to_all | solution.py:46
  241.2 9.1 %gather_fusion.1 = f32[256,4096]{1,0:T(8,128)} fusion(f32[512,4096]{1,0:T(8,128)} %bitcast.2, s32[1024]{0:T(1024)S(1)} %pad_clamp_fusion), kind=kCustom, calls=%fused_computation.1 | custom fusion | bytes 8389632 | tf_op jit(solution)/shard_map/gather | solution.py:53
  250.3 7.7 %fusion.80 = f32[256,256]{1,0:T(8,128)} fusion(f32[256,4096]{1,0:T(8,128)} %gather_fusion.1), kind=kOutput, calls=%fused_computation.168 | convolution fusion | flops 3221225472 | bytes 4456448 | tf_op jit(solution)/shard_map/dot_general | solution.py:54
  258.9 56.0 %all-reduce.5.cloned.1.call-done = f32[256,256]{1,0:T(8,128)} async-done(((f32[256,256]{1,0:T(8,128)}), f32[256,256]{1,0:T(8,128)}) %all-reduce.5.cloned.1.call-update) | async-done | bytes 262160 | tf_op jit(solution)/shard_map/psum | solution.py:55
  315.0 1.5 fusion.81
  316.6 11.7 %cholesky.214 = f32[128,128]{1,0:T(8,128)S(1)} custom-call(f32[128,128]{1,0:T(8,128)S(1)} %cholesky.346), custom_call_target="Cholesky" | custom-call | tf_op jit(solution)/shard_map/jit(cholesky)/cholesky | solution.py:18
  328.4 9.8 %custom-call.17 = f32[1,128,128]{1,2,0:T(8,128)S(1)} custom-call(f32[1,128,128]{2,1,0:T(8,128)S(1)} %get-tuple-element.94), custom_call_target="InvertDiagBlocksLowerTriangular" | custom-call | tf_op jit(solution)/shard_map/jit(cholesky)/cholesky | solution.py:18
  338.7 11.7 %cholesky.231 = f32[128,128]{1,0:T(8,128)S(1)} custom-call(f32[128,128]{1,0:T(8,128)S(1)} %convolution_subtract_fusion.6), custom_call_target="Cholesky" | custom-call | tf_op jit(solution)/shard_map/jit(cholesky)/cholesky | solution.py:18
  350.5 0.7 compare_reduce_fusion.6
  352.5 4.0 while.8
  352.6 0.6 fusion.124
  353.2 1.3 bitcast_dynamic-update-slice_fusion.8
  354.6 0.6 fusion.124
  355.2 1.3 bitcast_dynamic-update-slice_fusion.8
  356.6 20.1 %custom-call.18 = f32[2,128,128]{1,2,0:T(8,128)S(1)} custom-call(f32[2,128,128]{2,1,0:T(8,128)S(1)} %get-tuple-element.33), custom_call_target="InvertDiagBlocksLowerTriangular" | custom-call | tf_op jit(solution)/shard_map/jit(_solve_triangular)/triangular_solve | solution.py:19
  379.6 11.7 %cholesky.248 = f32[128,128]{1,0:T(8,128)S(1)} custom-call(f32[128,128]{1,0:T(8,128)S(1)} %cholesky.349), custom_call_target="Cholesky" | custom-call | tf_op jit(solution)/shard_map/jit(cholesky)/cholesky | solution.py:18
  391.3 9.8 %custom-call.19 = f32[1,128,128]{1,2,0:T(8,128)S(1)} custom-call(f32[1,128,128]{2,1,0:T(8,128)S(1)} %get-tuple-element.90), custom_call_target="InvertDiagBlocksLowerTriangular" | custom-call | tf_op jit(solution)/shard_map/jit(cholesky)/cholesky | solution.py:18
  401.6 11.9 %cholesky.265 = f32[128,128]{1,0:T(8,128)S(1)} custom-call(f32[128,128]{1,0:T(8,128)S(1)} %convolution_subtract_fusion.5), custom_call_target="Cholesky" | custom-call | tf_op jit(solution)/shard_map/jit(cholesky)/cholesky | solution.py:18
  413.5 0.7 compare_reduce_fusion.5
  414.2 0.6 compare_reduce_fusion.4
  416.2 4.1 while.9
  416.2 0.7 fusion.125
  416.9 1.3 bitcast_dynamic-update-slice_fusion.9
  418.2 0.7 fusion.125
  418.9 1.3 bitcast_dynamic-update-slice_fusion.9
  420.3 19.7 %custom-call.20 = f32[2,128,128]{1,2,0:T(8,128)S(1)} custom-call(f32[2,128,128]{2,1,0:T(8,128)S(1)} %get-tuple-element.34), custom_call_target="InvertDiagBlocksLowerTriangular" | custom-call | tf_op jit(solution)/shard_map/jit(_solve_triangular)/triangular_solve | solution.py:19
  441.3 5.5 fusion.83
  447.1 3.2 collective-permute-start
  450.3 92.2 %collective-permute-done = f32[128,4096]{1,0:T(8,128)S(1)} collective-permute-done((f32[128,4096]{1,0:T(8,128)S(1)}, f32[128,4096]{1,0:T(8,128)S(1)}, u32[]{:S(2)}, u32[]{:S(2)}) %collective-permute-start) | collective-permute-done | bytes 2097184 | tf_op jit(solution)/shard_map/ppermute | solution.py:10
  542.5 1.3 copy-done.2
  543.8 4.2 fusion.1
  548.1 48.0 %all-reduce.7.cloned.1.call-done = f32[256,256]{1,0:T(8,128)} async-done(((f32[256,256]{1,0:T(8,128)}), f32[256,256]{1,0:T(8,128)}) %all-reduce.7.cloned.1.call-update) | async-done | bytes 262160 | tf_op jit(solution)/shard_map/psum | solution.py:65
  596.1 1.5 fusion.84
  597.8 11.7 %cholesky.282 = f32[128,128]{1,0:T(8,128)S(1)} custom-call(f32[128,128]{1,0:T(8,128)S(1)} %cholesky.352), custom_call_target="Cholesky" | custom-call | tf_op jit(solution)/shard_map/jit(cholesky)/cholesky | solution.py:18
  609.5 9.8 %custom-call.21 = f32[1,128,128]{1,2,0:T(8,128)S(1)} custom-call(f32[1,128,128]{2,1,0:T(8,128)S(1)} %get-tuple-element.86), custom_call_target="InvertDiagBlocksLowerTriangular" | custom-call | tf_op jit(solution)/shard_map/jit(cholesky)/cholesky | solution.py:18
  619.8 12.1 %cholesky.299 = f32[128,128]{1,0:T(8,128)S(1)} custom-call(f32[128,128]{1,0:T(8,128)S(1)} %convolution_subtract_fusion.4), custom_call_target="Cholesky" | custom-call | tf_op jit(solution)/shard_map/jit(cholesky)/cholesky | solution.py:18
  631.9 0.6 compare_reduce_fusion.3
  632.6 0.6 compare_reduce_fusion.2
  634.6 4.0 while.10
  634.6 0.6 fusion.126
  635.2 1.4 bitcast_dynamic-update-slice_fusion.10
  636.6 0.6 fusion.126
  637.2 1.4 bitcast_dynamic-update-slice_fusion.10
  638.6 19.7 %custom-call.22 = f32[2,128,128]{1,2,0:T(8,128)S(1)} custom-call(f32[2,128,128]{2,1,0:T(8,128)S(1)} %get-tuple-element.35), custom_call_target="InvertDiagBlocksLowerTriangular" | custom-call | tf_op jit(solution)/shard_map/jit(_solve_triangular)/triangular_solve | solution.py:19
  661.1 11.7 %cholesky.316 = f32[128,128]{1,0:T(8,128)S(1)} custom-call(f32[128,128]{1,0:T(8,128)S(1)} %cholesky.355), custom_call_target="Cholesky" | custom-call | tf_op jit(solution)/shard_map/jit(cholesky)/cholesky | solution.py:18
  672.8 9.8 %custom-call.23 = f32[1,128,128]{1,2,0:T(8,128)S(1)} custom-call(f32[1,128,128]{2,1,0:T(8,128)S(1)} %get-tuple-element.82), custom_call_target="InvertDiagBlocksLowerTriangular" | custom-call | tf_op jit(solution)/shard_map/jit(cholesky)/cholesky | solution.py:18
  683.1 11.9 %cholesky.333 = f32[128,128]{1,0:T(8,128)S(1)} custom-call(f32[128,128]{1,0:T(8,128)S(1)} %convolution_subtract_fusion.3), custom_call_target="Cholesky" | custom-call | tf_op jit(solution)/shard_map/jit(cholesky)/cholesky | solution.py:18
  695.0 0.6 compare_reduce_fusion.1
  695.7 0.6 compare_reduce_fusion
  697.6 3.9 while.11
  698.3 1.4 bitcast_dynamic-update-slice_fusion.11
  700.2 1.4 bitcast_dynamic-update-slice_fusion.11
  701.6 19.7 %custom-call.24 = f32[2,128,128]{1,2,0:T(8,128)S(1)} custom-call(f32[2,128,128]{2,1,0:T(8,128)S(1)} %get-tuple-element.36), custom_call_target="InvertDiagBlocksLowerTriangular" | custom-call | tf_op jit(solution)/shard_map/jit(_solve_triangular)/triangular_solve | solution.py:19
  722.6 7.6 %fusion = f32[256,4096]{1,0:T(8,128)} fusion(f32[256,256]{1,0:T(8,128)S(1)} %fusion.6, f32[128,4096]{1,0:T(8,128)} %copy-done.2, f32[128,4096]{1,0:T(8,128)S(1)} %get-tuple-element.77), kind=kOutput, calls=%fused_computation.14 | convolution fusion | flops 3222274048 | bytes 8650752 | tf_op jit(solution)/shard_map/dot_general | solution.py:67
  (100 shorter events, 13.6 us)
Async XLA Ops:
  9.5 32.9 %all-to-all-start.1 = ((s32[64,8,1]{1,2,0:T(1,128)}), s32[64,8,1]{1,2,0:T(1,128)S(1)}, u32[]{:S(2)}, u32[]{:S(2)}) async-start(s32[64,8,1]{1,2,0:T(1,128)} %bitcast.3), calls=%async_computation.1 | async-start | bytes 65536 | tf_op jit(solution)/shard_map/all_to_all | solution.py:47
  42.4 198.8 %all-to-all-start = ((f32[64,8,4096]{2,1,0:T(8,128)}), f32[64,8,4096]{2,1,0:T(8,128)}, u32[]{:S(2)}, u32[]{:S(2)}) async-start(f32[64,8,4096]{2,1,0:T(8,128)} %bitcast.156), calls=%async_computation | async-start | bytes 16777216 | tf_op jit(solution)/shard_map/all_to_all | solution.py:46
  55.4 259.5 %all-reduce.5.cloned.1.call-start = ((), (), s32[]{:S(2)}) async-start(), calls=%async_computation.2 | async-start | bytes 524288 | tf_op jit(solution)/shard_map/psum | solution.py:55
  258.0 338.1 %all-reduce.7.cloned.1.call-start = ((), (), s32[]{:S(2)}) async-start(), calls=%async_computation.3 | async-start | bytes 524288 | tf_op jit(solution)/shard_map/psum | solution.py:65
  315.0 61.8 %copy-start = (f32[256,256]{1,0:T(8,128)S(1)}, f32[256,256]{1,0:T(8,128)}, u32[]{:S(2)}) copy-start(f32[256,256]{1,0:T(8,128)} %all-reduce.5.cloned.1.call-done) | copy-start | bytes 786436
  447.1 95.4 %collective-permute-start = (f32[128,4096]{1,0:T(8,128)S(1)}, f32[128,4096]{1,0:T(8,128)S(1)}, u32[]{:S(2)}, u32[]{:S(2)}) collective-permute-start(f32[128,4096]{1,0:T(8,128)S(1)} %get-tuple-element.78), channel_id=1, source_target_pairs={{0,128},{4,132},{8,136},{12,140},{16,144},{20,148},{24,152},{28,15... | collective-permute-start | bytes 6291464 | tf_op jit(solution)/shard_map/ppermute | solution.py:10
  542.5 1.4 copy-start.2
  596.1 62.2 %copy-start.1 = (f32[256,256]{1,0:T(8,128)S(1)}, f32[256,256]{1,0:T(8,128)}, u32[]{:S(2)}) copy-start(f32[256,256]{1,0:T(8,128)} %all-reduce.7.cloned.1.call-done) | copy-start | bytes 786436
Sparse Core Ops, SparseCore 0:
  258.1 56.7 all-reduce.4
  548.2 47.8 all-reduce.6
where the time goes:
time: 745 us; the launch traced here: 737 us
  waiting for transfers between devices  378 us (51%)
  other arithmetic  220 us (30%)
  local copies, waits for them, and re-layouts  49.8 us (7%)
  matrix products  37.1 us (5%)
  starting transfers between devices  32.1 us (4%)
  between operations  20 us (3%)
    all_to_all x1, waiting for transfers between devices, body(): lax.all_to_all(outgoing, 'col', split_axis=0, concat_axis=0, tiled=True)  182 us
    another operation x27, other arithmetic, orthogonal_steps(): factor = jnp.linalg.cholesky(squared)  139 us
    ppermute x1, waiting for transfers between devices, from_partner(): lax.ppermute(array, axis, [(i, i ^ 1 << distance) for i in range(lax.axis...  92.2 us
    another operation x9, other arithmetic, orthogonal_steps(): jax.scipy.linalg.solve_triangular(factor, pair_gram, lower=True)  79.3 us
    psum x1, waiting for transfers between devices, body(): pair_gram = lax.psum(partial_value, 'row')  56 us
    psum x1, waiting for transfers between devices, body(): second_gram = lax.psum(second_partial, 'row')  48 us
    another operation x29, local copies, waits for them, and re-layouts, orthogonal_steps(): jax.scipy.linalg.solve_triangular(factor, pair_gram, lower=True)  15.9 us
    all_to_all x1, starting transfers between devices, body(): lax.all_to_all(position_of_slot, 'col', split_axis=0, concat_axis=0, tile...  15.6 us
  transfers between devices with their start and end apart: 5, of which 4 were waited for; matrix products, arithmetic and copies ran while one was open for 3% of the time, Pallas kernels for 0%

commit v1 on v0

v1 whole, which is shorter than its diff:
```python
import functools

import jax
import jax.numpy as jnp
from jax import lax
from jax.experimental import pallas as pl
from jax.experimental.pallas import tpu as pltpu
from jax.sharding import PartitionSpec as P

CHUNKS = 8
BLOCK = 64
F32 = jnp.float32
BF16 = jnp.bfloat16
MESH = pl.DeviceIdType.MESH
HIGHEST = lax.Precision.HIGHEST


def split3(value):
    high = value.astype(BF16)
    rest = value - high.astype(F32)
    middle = rest.astype(BF16)
    low = (rest - middle.astype(F32)).astype(BF16)
    return high, middle, low


def select_rows(one_hot, value):
    high, middle, low = split3(value)
    dot = functools.partial(jnp.dot, one_hot, preferred_element_type=F32)
    return (dot(high) + dot(middle)) + dot(low)


def dot_f32(a, b, dims=((1,), (0,))):
    return lax.dot_general(a, b, (dims, ((), ())), precision=HIGHEST, preferred_element_type=F32)


def gram_update(rows):
    high, middle, low = split3(rows)
    nt = (((1,), (1,)), ((), ()))
    dot = functools.partial(lax.dot_general, dimension_numbers=nt, preferred_element_type=F32)
    cross = dot(middle, high) + dot(low, high)
    return dot(high, high) + dot(middle, middle) + cross, cross


def exchange_kernel(
    peers, x_ref, slot_source_ref, row_slot_ref,
    own_hbm, other_hbm, both_hbm, tri_ref,
    out_buf, in_buf, both_buf, other_buf, gram_buf, cross_buf,
    out_sem, in_sem, z_out_sem, z_in_sem, write_sem,
):
    col = lax.axis_index("col")
    side = col // peers
    me = col % peers
    mirror = lax.rem(col + peers, 2 * peers)
    half = CHUNKS // 2
    slots = out_buf.shape[2]
    width = out_buf.shape[3]
    rows = other_buf.shape[1]

    barrier = pltpu.get_barrier_semaphore()

    def greet(step, carry):
        peer = side * peers + lax.rem(me + step, peers)
        pl.semaphore_signal(barrier, inc=1, device_id={"col": peer}, device_id_type=MESH)
        return carry

    lax.fori_loop(1, peers, greet, 0)
    pl.semaphore_signal(barrier, inc=1, device_id={"col": mirror}, device_id_type=MESH)
    pl.semaphore_wait(barrier, peers)

    place = lax.broadcasted_iota(jnp.int32, (peers * slots, rows), 1)
    pack = (slot_source_ref[...] == place).astype(BF16)

    def send_chunk(index, carry):
        chunk = lax.rem((1 - side) * half + index, CHUNKS)
        piece = x_ref[:, pl.ds(pl.multiple_of(chunk * width, width), width)]
        packed = select_rows(pack, piece).reshape(peers, slots, width)
        out_buf[index] = packed

        def send(step, inner):
            peer = lax.rem(me + step, peers)
            pltpu.make_async_remote_copy(
                src_ref=out_buf.at[index, peer],
                dst_ref=in_buf.at[index, me],
                send_sem=out_sem.at[index],
                recv_sem=in_sem.at[index],
                device_id={"col": side * peers + peer},
                device_id_type=MESH,
            ).start()
            return inner

        lax.fori_loop(1, peers, send, 0)
        in_buf[index, me] = out_buf[index, me]
        return carry

    lax.fori_loop(0, CHUNKS, send_chunk, 0)

    slot = lax.broadcasted_iota(jnp.int32, (rows, peers * slots), 1)
    compact = (row_slot_ref[...] == slot).astype(BF16)

    def arrived(index):
        pltpu.make_async_copy(
            in_buf.at[index, pl.ds(0, peers - 1)], in_buf.at[index, pl.ds(0, peers - 1)], in_sem.at[index]
        ).wait()
        return select_rows(compact, in_buf[index].reshape(peers * slots, width))

    def cross_copy(index):
        return pltpu.make_async_remote_copy(
            src_ref=other_buf.at[index],
            dst_ref=both_buf.at[index, pl.ds(pl.multiple_of(side * rows, rows), rows)],
            send_sem=z_out_sem.at[index],
            recv_sem=z_in_sem.at[index],
            device_id={"col": mirror},
            device_id_type=MESH,
        )

    def write_other(index):
        return pltpu.make_async_copy(other_buf.at[index], other_hbm.at[index], write_sem.at[index])

    def write_own(index):
        source = both_buf.at[index, pl.ds(pl.multiple_of(side * rows, rows), rows)]
        return pltpu.make_async_copy(source, own_hbm.at[index], write_sem.at[half + index])

    def write_both(index):
        return pltpu.make_async_copy(both_buf.at[index], both_hbm.at[index], write_sem.at[2 * half + index])

    def cross_chunk(index, carry):
        other_buf[index] = arrived(index)
        cross_copy(index).start()
        write_other(index).start()
        return carry

    lax.fori_loop(0, half, cross_chunk, 0)

    def keep_chunk(index, carry):
        both_buf[index, pl.ds(pl.multiple_of(side * rows, rows), rows)] = arrived(half + index)
        write_own(index).start()
        return carry

    lax.fori_loop(0, half, keep_chunk, 0)

    gram_buf[...] = jnp.zeros_like(gram_buf)
    cross_buf[...] = jnp.zeros_like(cross_buf)

    def gram_chunk(index, carry):
        cross_copy(index).wait_recv()
        write_both(index).start()
        total, cross = gram_update(both_buf[index])
        gram_buf[...] += total
        cross_buf[...] += cross
        return carry

    lax.fori_loop(0, half, gram_chunk, 0)
    gram = gram_buf[...] + cross_buf[...].T
    quarter = rows // 2
    place = 0
    for i in range(4):
        for j in range(i + 1):
            tri_ref[place * quarter:(place + 1) * quarter, :] = gram[
                i * quarter:(i + 1) * quarter, j * quarter:(j + 1) * quarter
            ]
            place += 1

    def finish(index, carry):
        cross_copy(index).wait_send()
        write_other(index).wait()
        write_own(index).wait()
        write_both(index).wait()
        return carry

    lax.fori_loop(0, half, finish, 0)

    def sent(index, carry):
        pltpu.make_async_copy(
            out_buf.at[index, pl.ds(0, peers - 1)], out_buf.at[index, pl.ds(0, peers - 1)], out_sem.at[index]
        ).wait()
        return carry

    lax.fori_loop(0, CHUNKS, sent, 0)


def exchange(x, slot_source, row_slot, peers):
    rows, columns = x.shape
    width = columns // CHUNKS
    half = CHUNKS // 2
    slots = slot_source.shape[0] // peers
    any_space = pl.BlockSpec(memory_space=pl.ANY)
    vmem = pl.BlockSpec(memory_space=pltpu.VMEM)
    return pl.pallas_call(
        functools.partial(exchange_kernel, peers),
        out_shape=[
            jax.ShapeDtypeStruct((half, rows, width), F32),
            jax.ShapeDtypeStruct((half, rows, width), F32),
            jax.ShapeDtypeStruct((half, 2 * rows, width), F32),
            jax.ShapeDtypeStruct((10 * rows // 2, rows // 2), F32),
        ],
        in_specs=[vmem, vmem, vmem],
        out_specs=[any_space, any_space, any_space, vmem],
        scratch_shapes=[
            pltpu.VMEM((CHUNKS, peers, slots, width), F32),
            pltpu.VMEM((CHUNKS, peers, slots, width), F32),
            pltpu.VMEM((half, 2 * rows, width), F32),
            pltpu.VMEM((half, rows, width), F32),
            pltpu.VMEM((2 * rows, 2 * rows), F32),
            pltpu.VMEM((2 * rows, 2 * rows), F32),
            pltpu.SemaphoreType.DMA((CHUNKS,)),
            pltpu.SemaphoreType.DMA((CHUNKS,)),
            pltpu.SemaphoreType.DMA((half,)),
            pltpu.SemaphoreType.DMA((half,)),
            pltpu.SemaphoreType.DMA((3 * half,)),
        ],
        compiler_params=pltpu.CompilerParams(
            collective_id=0, has_side_effects=True, vmem_limit_bytes=56 << 20
        ),
        cost_estimate=pl.CostEstimate(flops=10**10, bytes_accessed=10**8, transcendentals=0),
        name="exchange",
    )(x, slot_source, row_slot)


def sum_kernel(peers, row_count, tri_ref, out_ref, parts, total, out_sem, in_sem, back_out_sem, back_in_sem):
    col = lax.axis_index("col")
    side = col // peers
    row = lax.axis_index("row")
    count = 2 * row_count
    me = side * row_count + row
    size = parts.shape[1]

    def device(index):
        return {"col": (index // row_count) * peers + col % peers, "row": index % row_count}

    barrier = pltpu.get_barrier_semaphore()
    for step in range(1, count):
        pl.semaphore_signal(barrier, inc=1, device_id=device(lax.rem(me + step, count)), device_id_type=MESH)
    pl.semaphore_wait(barrier, count - 1)

    def piece(index):
        return pl.ds(pl.multiple_of(index * size, size), size)

    for step in range(1, count):
        to = lax.rem(me + step, count)
        pltpu.make_async_remote_copy(
            src_ref=tri_ref.at[piece(to)], dst_ref=parts.at[me], send_sem=out_sem, recv_sem=in_sem,
            device_id=device(to), device_id_type=MESH,
        ).start()
    parts[me] = tri_ref[piece(me), :]
    several = parts.at[pl.ds(0, count - 1)]
    pltpu.make_async_copy(several, several, in_sem).wait()
    value = parts[0]
    for index in range(1, count):
        value = value + parts[index]
    total[me] = value
    for step in range(1, count):
        to = lax.rem(me + step, count)
        pltpu.make_async_remote_copy(
            src_ref=total.at[me], dst_ref=total.at[me], send_sem=back_out_sem, recv_sem=back_in_sem,
            device_id=device(to), device_id_type=MESH,
        ).start()
    several = total.at[pl.ds(0, count - 1)]
    pltpu.make_async_copy(several, several, back_in_sem).wait()
    out_ref[...] = total[...].reshape(out_ref.shape)
    pltpu.make_async_copy(several, several, out_sem).wait()
    pltpu.make_async_copy(several, several, back_out_sem).wait()


def sum_over_devices(tri, peers, row_count):
    count = 2 * row_count
    size = tri.shape[0] // count
    vmem = pl.BlockSpec(memory_space=pltpu.VMEM)
    return pl.pallas_call(
        functools.partial(sum_kernel, peers, row_count),
        out_shape=jax.ShapeDtypeStruct(tri.shape, F32),
        in_specs=[vmem],
        out_specs=vmem,
        scratch_shapes=[
            pltpu.VMEM((count, size, tri.shape[1]), F32),
            pltpu.VMEM((count, size, tri.shape[1]), F32),
            pltpu.SemaphoreType.DMA,
            pltpu.SemaphoreType.DMA,
            pltpu.SemaphoreType.DMA,
            pltpu.SemaphoreType.DMA,
        ],
        compiler_params=pltpu.CompilerParams(collective_id=1, has_side_effects=True),
        cost_estimate=pl.CostEstimate(flops=10**9, bytes_accessed=10**8, transcendentals=0),
        name="sum_over_devices",
    )(tri)


def inverse_factors(blocks):
    size = BLOCK
    groups = size // 8
    sublane = lax.broadcasted_iota(jnp.int32, (8, 2 * size), 0)
    lane = lax.broadcasted_iota(jnp.int32, (8, 2 * size), 1)
    held = []
    for block in blocks:
        parts = []
        for g in range(groups):
            unit = (lane == sublane + (size + 8 * g)).astype(F32)
            left = jnp.concatenate([block[8 * g:8 * g + 8, :], jnp.zeros((8, size), F32)], axis=1)
            parts.append(left + unit)
        held.append(parts)
    for j in range(size):
        first, within = divmod(j, 8)
        for parts in held:
            row = parts[first][within:within + 1, :]
            scaled = row * (1.0 / row[:, j:j + 1])
            for g in range(first, groups):
                column = parts[g][:, j:j + 1]
                if g == first:
                    column = jnp.where(sublane[:, :1] > within, column, 0.0)
                parts[g] = parts[g] - column * scaled
    result = []
    for parts in held:
        rows = []
        for g in range(groups):
            pivot = jnp.sum(jnp.where(lane == sublane + 8 * g, parts[g], 0.0), axis=1, keepdims=True)
            rows.append(parts[g] * lax.rsqrt(pivot))
        result.append(jnp.concatenate(rows, axis=0)[:, size:])
    return result


def eliminate(work_refs, width):
    size = work_refs[0].shape[0]
    for start in range(0, size, BLOCK):
        stop = start + BLOCK
        inverses = inverse_factors([work[start:stop, start:stop] for work in work_refs])
        base = start - start % 128
        for work, inverse in zip(work_refs, inverses):
            top = dot_f32(inverse, work[start:stop, base:width])
            work[start:stop, base:width] = top
            if stop < size:
                below = top[:, stop - base:size - base]
                work[stop:size, base:width] = work[stop:size, base:width] - dot_f32(below, top, ((0,), (0,)))


def orthogonal_steps(grams, work_refs):
    size = grams[0].shape[0]
    row = lax.broadcasted_iota(jnp.int32, (size, size), 0)
    column = lax.broadcasted_iota(jnp.int32, (size, size), 1)
    for gram, work in zip(grams, work_refs):
        trace = jnp.sum(jnp.where(row == column, gram, 0.0))
        gram = gram * (size / trace)
        work[:, :size] = dot_f32(gram, gram)
    eliminate(work_refs, size)
    for work in work_refs:
        factor = jnp.where(row <= column, work[:, :size], 0.0)
        work[:, :size] = dot_f32(factor, factor, ((1,), (1,)))
        work[:, size:] = factor
    eliminate(work_refs, 2 * size)
    return [work[:, size:] for work in work_refs]


def rotation_kernel(tri_ref, position_ref, own_slot_ref, partner_slot_ref, weight_ref, gram_buf, work_a, work_b):
    quarter = tri_ref.shape[1]
    size = 2 * quarter
    place = 0
    for i in range(4):
        for j in range(i + 1):
            block = tri_ref[place * quarter:(place + 1) * quarter, :]
            gram_buf[i * quarter:(i + 1) * quarter, j * quarter:(j + 1) * quarter] = block
            if i != j:
                gram_buf[j * quarter:(j + 1) * quarter, i * quarter:(i + 1) * quarter] = block.T
            place += 1
    slot = lax.broadcasted_iota(jnp.int32, (2 * size, 2 * size), 0)
    place_of = (slot == position_ref[...]).astype(BF16)
    half_way = select_rows(place_of, gram_buf[...])
    gram_buf[...] = select_rows(place_of, half_way.T)
    own = gram_buf[:size, :size]
    partner = gram_buf[size:, size:]
    between = gram_buf[:size, size:]
    own_turn, partner_turn = orthogonal_steps([own, partner], [work_a, work_b])
    own_part = jnp.where(own_slot_ref[0] == 0, own_turn[quarter:], own_turn[:quarter])
    partner_part = jnp.where(partner_slot_ref[0] == 0, partner_turn[:quarter], partner_turn[quarter:])
    nt = ((1,), (1,))
    upper = dot_f32(dot_f32(own_part, own), own_part, nt)
    lower = dot_f32(dot_f32(partner_part, partner), partner_part, nt)
    mixed = dot_f32(dot_f32(own_part, between), partner_part, nt)
    gram_buf[:quarter, :quarter] = upper
    gram_buf[quarter:size, quarter:size] = lower
    gram_buf[:quarter, quarter:size] = mixed
    gram_buf[quarter:size, :quarter] = mixed.T
    second = gram_buf[:size, :size]
    (last,) = orthogonal_steps([0.5 * (second + second.T)], [work_a])
    gram_buf[:size, :size] = dot_f32(last[:, :quarter], own_part)
    gram_buf[:size, size:] = dot_f32(last[:, quarter:], partner_part)
    high, middle, low = split3(gram_buf[:size, :])
    dot = functools.partial(jnp.dot, preferred_element_type=F32)
    weight_ref[...] = (dot(high, place_of) + dot(middle, place_of)) + dot(low, place_of)


def rotations(tri, position, own_slot, partner_slot):
    size = 2 * tri.shape[1]
    vmem = pl.BlockSpec(memory_space=pltpu.VMEM)
    smem = pl.BlockSpec(memory_space=pltpu.SMEM)
    return pl.pallas_call(
        rotation_kernel,
        out_shape=jax.ShapeDtypeStruct((size, 2 * size), F32),
        in_specs=[vmem, vmem, smem, smem],
        out_specs=vmem,
        scratch_shapes=[
            pltpu.VMEM((2 * size, 2 * size), F32),
            pltpu.VMEM((size, 2 * size), F32),
            pltpu.VMEM((size, 2 * size), F32),
        ],
        compiler_params=pltpu.CompilerParams(vmem_limit_bytes=32 << 20),
        cost_estimate=pl.CostEstimate(flops=6 * 10**10, bytes_accessed=10**8, transcendentals=0),
        name="rotations",
    )(tri, position, own_slot, partner_slot)


def product3(a, b):
    a_high = a.astype(BF16)
    a_low = (a - a_high.astype(F32)).astype(BF16)
    b_high = b.astype(BF16)
    b_low = (b - b_high.astype(F32)).astype(BF16)
    dot = functools.partial(jnp.dot, preferred_element_type=F32)
    return dot(a_high, b_high) + (dot(a_high, b_low) + dot(a_low, b_high))


def apply_both_kernel(start_ref, weight_ref, both_ref, out_ref):
    out_ref[...] = product3(weight_ref[...], both_ref[0])


def apply_both(start, weight, both, columns):
    chunks, rows, width = both.shape
    size = weight.shape[0]
    return pl.pallas_call(
        apply_both_kernel,
        grid_spec=pltpu.PrefetchScalarGridSpec(
            num_scalar_prefetch=1,
            grid=(chunks,),
            in_specs=[
                pl.BlockSpec((size, rows), lambda i, s: (0, 0)),
                pl.BlockSpec((1, rows, width), lambda i, s: (i, 0, 0)),
            ],
            out_specs=pl.BlockSpec((size, width), lambda i, s: (0, s[0] * chunks + i)),
        ),
        out_shape=jax.ShapeDtypeStruct((size, columns), F32),
        cost_estimate=pl.CostEstimate(flops=10**10, bytes_accessed=10**7, transcendentals=0),
        compiler_params=pltpu.CompilerParams(vmem_limit_bytes=32 << 20),
        name="apply_both",
    )(start, weight, both)


def apply_rest_kernel(start_ref, weight_ref, own_ref, mirror_ref, partial_ref, out_ref):
    rows = own_ref.shape[1]
    side = start_ref[0]
    own_weight = jnp.where(side == 0, weight_ref[:, :rows], weight_ref[:, rows:])
    mirror_weight = jnp.where(side == 0, weight_ref[:, rows:], weight_ref[:, :rows])
    out_ref[...] = product3(own_weight, own_ref[0]) + product3(mirror_weight, mirror_ref[0])


def apply_rest(start, weight, own, mirror, partial):
    chunks, rows, width = own.shape
    size = weight.shape[0]
    return pl.pallas_call(
        apply_rest_kernel,
        grid_spec=pltpu.PrefetchScalarGridSpec(
            num_scalar_prefetch=1,
            grid=(chunks,),
            in_specs=[
                pl.BlockSpec((size, 2 * rows), lambda i, s: (0, 0)),
                pl.BlockSpec((1, rows, width), lambda i, s: (i, 0, 0)),
                pl.BlockSpec((1, rows, width), lambda i, s: (i, 0, 0)),
                pl.BlockSpec(memory_space=pl.ANY),
            ],
            out_specs=pl.BlockSpec((size, width), lambda i, s: (0, (1 - s[0]) * chunks + i)),
        ),
        out_shape=jax.ShapeDtypeStruct(partial.shape, F32),
        input_output_aliases={4: 0},
        cost_estimate=pl.CostEstimate(flops=10**10, bytes_accessed=10**7, transcendentals=0),
        compiler_params=pltpu.CompilerParams(vmem_limit_bytes=32 << 20),
        name="apply_rest",
    )(start, weight, own, mirror, partial)


def slot_tables(dest_ids, col, peers, slots):
    rows = dest_ids.shape[0]
    count = 2 * peers
    local = jnp.arange(rows, dtype=jnp.int32)
    target = dest_ids // rows
    peer = target % peers
    earlier = (peer[:, None] == peer[None, :]) & (local[None, :] < local[:, None])
    rank = jnp.sum(earlier.astype(jnp.int32), axis=1)
    wanted = jnp.arange(peers * slots, dtype=jnp.int32)
    slot = peer * slots + rank
    slot_source = jnp.max(jnp.where(slot[None, :] == wanted[:, None], local[None, :], -1), axis=1)
    offset = (target - col) % peers
    amount = jnp.sum((offset[None, :] == jnp.arange(peers, dtype=jnp.int32)[:, None]).astype(jnp.int32), axis=1)
    sender = jnp.arange(peers, dtype=jnp.int32)
    sender_offset = (col - sender) % peers
    from_sender = jnp.sum(
        jnp.where(sender_offset[:, None] == jnp.arange(peers, dtype=jnp.int32)[None, :], amount[None, :], 0), axis=1
    )
    base = jnp.sum(jnp.where(sender[None, :] < sender[:, None], from_sender[None, :], 0), axis=1)
    within = jnp.arange(slots, dtype=jnp.int32)
    row_of_slot = jnp.where(within[None, :] < from_sender[:, None], base[:, None] + within[None, :], -1).reshape(-1)
    row_slot = jnp.max(jnp.where(row_of_slot[None, :] == local[:, None], wanted[None, :], -1), axis=1)
    return slot_source[:, None], row_slot[:, None]


def final_positions(every_id, col, peers, slots):
    devices, rows = every_id.shape
    target = every_id // rows
    mine = target % peers == col % peers
    place = jnp.where(target == col, 0, rows) + every_id % rows
    local = jnp.arange(rows, dtype=jnp.int32)
    before = (local[:, None] < local[None, :]).astype(BF16)
    rank = jnp.dot(mine.astype(BF16), before, preferred_element_type=F32).astype(jnp.int32)
    within = jnp.arange(slots, dtype=jnp.int32)
    held = jnp.max(
        jnp.where(mine[:, None, :] & (rank[:, None, :] == within[None, :, None]), place[:, None, :], -1), axis=2
    )
    amount = jnp.sum(mine.astype(jnp.int32), axis=1)
    device = jnp.arange(devices, dtype=jnp.int32)
    base = jnp.sum(jnp.where(device[None, :] < device[:, None], amount[None, :], 0), axis=1)
    row_of = jnp.where(held >= 0, base[:, None] + within[None, :], -1).reshape(-1)
    wanted = jnp.arange(2 * rows, dtype=jnp.int32)
    position = jnp.max(jnp.where(row_of[:, None] == wanted[None, :], held.reshape(-1)[:, None], -1), axis=0)
    return position[None, :]


def body(row_count, greens_matrix, dest_ids, send_slot):
    rows, columns = greens_matrix.shape
    count = lax.axis_size("col")
    peers = count // 2
    cap = max(2, 2 * rows // count)
    slots = 2 * cap
    col = lax.axis_index("col")
    every_id = lax.all_gather(dest_ids, "col")
    every_slot = lax.all_gather(send_slot, "col").reshape(-1)
    slot_source, row_slot = slot_tables(dest_ids, col, peers, slots)
    own, other, both, tri = exchange(greens_matrix, slot_source, row_slot, peers)
    mirror = lax.ppermute(own, "col", [(i, i ^ peers) for i in range(count)])
    tri = sum_over_devices(tri, peers, row_count)
    position = final_positions(every_id, col, peers, slots)
    device = jnp.arange(count, dtype=jnp.int32)
    partner_slot = jnp.sum(jnp.where(device == (col + peers) % count, every_slot, 0))[None]
    weight = rotations(tri, position, send_slot, partner_slot)
    side = (col // peers).astype(jnp.int32)[None]
    partial = apply_both(side, weight, both, columns)
    return apply_rest(side, weight, other, mirror, partial)


def solution(mesh):
    return jax.shard_map(
        functools.partial(body, mesh.shape["row"]),
        mesh=mesh,
        in_specs=(P("col", "row"), P("col"), P("col")),
        out_specs=P("col", "row"),
        check_vma=False,
    )
```

time: 745 us -> 504 us (0.68)
  the two profiles are of different devices: /device:TPU:1 before, /device:TPU:94 now
where the time goes in v1:
time: 504 us; the launch traced here: 499 us
  Pallas kernels  272 us (54%)
  blocking collectives  211 us (42%)
  local copies, waits for them, and re-layouts  6.54 us (1%)
    all_gather x1, blocking collectives, body(): every_id = lax.all_gather(dest_ids, 'col')  188 us
    pallas_call x1, Pallas kernels, exchange(): pl.pallas_call(functools.partial(exchange_kernel, peers), out_shape=[jax....  121 us
    pallas_call x1, Pallas kernels, rotations(): pl.pallas_call(rotation_kernel, out_shape=jax.ShapeDtypeStruct((size, 2 *...  106 us
    pallas_call x1, Pallas kernels, sum_over_devices(): pl.pallas_call(functools.partial(sum_kernel, peers, row_count), out_shape...  37.5 us
    unnamed x1, blocking collectives  22.9 us
  transfers between devices with their start and end apart: 1, of which 0 were waited for; matrix products, arithmetic and copies ran while one was open for 1% of the time, Pallas kernels for 30%

profile of v1, /device:TPU:94, one launch (start us, length us, event | category | flops | bytes accessed | tf_op | source)
XLA Modules:
  0.0 498.5 jit_solution(15463487631548952761)
XLA Ops:
  0.0 0.7 and_select_fusion
  0.7 0.1 convert_reduce_fusion.2
  0.8 0.2 select_reduce_fusion.6
  1.0 0.1 select_reduce_fusion.5
  1.1 0.2 convert_reduce_fusion
  1.3 0.2 select_reduce_fusion.3
  1.5 0.1 add_select_fusion.3
  1.6 0.1 select_n.118
  1.7 0.2 select_reduce_fusion.2
  1.8 0.8 copy.10.row_slot_ref
  2.6 0.9 copy.9.slot_source_ref
  3.5 0.0 copy-start.3
  3.5 0.0 copy-start.4
  3.5 121.4 %exchange.1 = (f32[4,256,512]{2,1,0:T(8,128)}, f32[4,256,512]{2,1,0:T(8,128)}, f32[4,512,512]{2,1,0:T(8,128)}, f32[1280,128]{1,0:T(8,128)}) custom-call(f32[256,4096]{1,0:T(8,128)} %x_ref.1, s32[512,1]{1,0:T(8,128)} %copy.9.slot_source_ref, s32[256,1]{1,0:T(8,128)} %copy.10.row_slot_ref), custom_call_target="tpu_custom_call" | custom-call | flops 10000000000 | bytes 100000000 | tf_op jit(solution)/shard_map/exchange/pallas_call | solution.py:188
  124.9 2.6 collective-permute-start
  127.5 0.0 copy-done.3
  127.5 188.4 %all-gather.2 = s32[64,1,256]{2,1,0:T(1,128)S(1)} all-gather(s32[1,1,256]{2,1,0:T(1,128)S(1)} %bitcast.41), channel_id=2, replica_groups=mesh['col'=64,'row'=4] {'col'}, dimensions={0}, use_global_device_ids=true | all-gather | bytes 66560 | tf_op jit(solution)/shard_map/all_gather | solution.py:528
  315.9 0.2 convert_reduce_fusion.1
  316.1 0.2 convolution_convert_fusion
  316.9 0.0 copy-done.4
  316.9 0.6 dynamic-slice
  317.5 0.8 dynamic-update-slice
  318.3 22.9 %all-reduce = s32[64]{0:T(128)S(1)} all-reduce(s32[64]{0:T(128)S(1)} %dynamic-update-slice), channel_id=3, replica_groups=mesh['col'=64,'row'=4] {'col'}, use_global_device_ids=true, to_apply=%add | all-reduce | flops 64 | bytes 512
  341.1 0.1 select_reduce_fusion.4
  341.2 0.1 iota_add_fusion
  341.3 0.1 add.98
  341.4 1.2 select_reduce_fusion.1
  342.6 0.1 reduce_max.41
  342.7 1.1 select_reduce_fusion
  343.8 37.5 %sum_over_devices.1.tri_ref = f32[1280,128]{1,0:T(8,128)} custom-call(f32[1280,128]{1,0:T(8,128)} %get-tuple-element.9.tri_ref), custom_call_target="tpu_custom_call" | custom-call | flops 1000000000 | bytes 100000000 | tf_op jit(solution)/shard_map/sum_over_devices/pallas_call | solution.py:268
  381.3 0.6 fusion.10
  382.0 0.0 copy-start
  382.0 1.1 copy-done
  383.0 106.2 %rotations.1.weight_ref = f32[256,512]{1,0:T(8,128)S(1)} custom-call(f32[1280,128]{1,0:T(8,128)S(1)} %copy-done, s32[1,512]{1,0:T(1,128)S(1)} %bitcast.39, s32[1]{0:T(128)S(6)} %copy.41.own_slot_ref, s32[1]{0:T(128)} %bitcast.6.partner_slot_ref), custom_call_target="tpu_custom_call" | custom-call | flops 60000002048 | bytes 100000000 | tf_op jit(solution)/shard_map/rotations/pallas_call | solution.py:393
  489.2 0.0 copy-start.1
  489.2 2.2 copy-done.1
  491.4 0.0 copy-start.2
  491.4 3.4 apply_both.1.partial_ref
  494.8 0.0 collective-permute-done.mirror_ref
  494.8 0.0 copy-done.2
  494.8 3.5 apply_rest.1
  (6 shorter events, 0.1 us)
Async XLA Ops:
  3.5 124.0 %copy-start.3 = (s32[256]{0:T(256)S(1)}, s32[256]{0:T(256)}, u32[]{:S(2)}) copy-start(s32[256]{0:T(256)} %param.4) | copy-start | bytes 3076
  3.5 313.4 %copy-start.4 = (u32[256]{0:T(256)S(1)}, u32[256]{0:T(256)}, u32[]{:S(2)}) copy-start(u32[256]{0:T(256)} %constant.112) | copy-start | bytes 3076
  124.9 369.9 %collective-permute-start = (f32[4,256,512]{2,1,0:T(8,128)}, f32[4,256,512]{2,1,0:T(8,128)S(1)}, u32[]{:S(2)}, u32[]{:S(2)}) collective-permute-start(f32[4,256,512]{2,1,0:T(8,128)} %get-tuple-element.11), channel_id=1, source_target_pairs={{0,128},{4,132},{8,136},{12,140},{16,144},{20,148},{24,152},{28,15... | collective-permute-start | bytes 6291464 | tf_op jit(solution)/shard_map/ppermute | solution.py:532
  382.0 1.1 copy-start
  489.2 2.2 copy-start.1
  491.4 3.4 copy-start.2

commit v2 on v1

--- a/solution.py
+++ b/solution.py
@@ -7,7 +7,8 @@
 from jax.experimental.pallas import tpu as pltpu
 from jax.sharding import PartitionSpec as P
 
-CHUNKS = 8
+CHUNKS = 16
+EARLY = 3
 BLOCK = 64
 F32 = jnp.float32
 BF16 = jnp.bfloat16
@@ -42,10 +43,11 @@
 
 
 def exchange_kernel(
-    peers, x_ref, slot_source_ref, row_slot_ref,
-    own_hbm, other_hbm, both_hbm, tri_ref,
-    out_buf, in_buf, both_buf, other_buf, gram_buf, cross_buf,
-    out_sem, in_sem, z_out_sem, z_in_sem, write_sem,
+    peers, row_count, x_ref, slot_source_ref, slot_place_ref, row_slot_ref, send_slot_ref,
+    own_hbm, other_hbm, both_hbm, early_hbm, tri_ref, note_ref,
+    out_buf, in_buf, both_buf, other_buf, early_buf, gram_buf, cross_buf, place_out, place_in, note_out, note_in,
+    tri_buf, parts, total,
+    out_sem, in_sem, z_out_sem, z_in_sem, write_sem, place_sem, note_sem, early_sem, sum_sem,
 ):
     col = lax.axis_index("col")
     side = col // peers
@@ -63,12 +65,20 @@
         pl.semaphore_signal(barrier, inc=1, device_id={"col": peer}, device_id_type=MESH)
         return carry
 
+    count = 2 * row_count
+    ring = side * row_count + lax.axis_index("row")
+
+    def ring_device(step):
+        index = lax.rem(ring + step, count)
+        return {"col": (index // row_count) * peers + me, "row": index % row_count}
+
     lax.fori_loop(1, peers, greet, 0)
-    pl.semaphore_signal(barrier, inc=1, device_id={"col": mirror}, device_id_type=MESH)
-    pl.semaphore_wait(barrier, peers)
-
-    place = lax.broadcasted_iota(jnp.int32, (peers * slots, rows), 1)
-    pack = (slot_source_ref[...] == place).astype(BF16)
+    for step in range(1, count):
+        pl.semaphore_signal(barrier, inc=1, device_id=ring_device(step), device_id_type=MESH)
+    pl.semaphore_wait(barrier, peers - 1 + count - 1)
+
+    place = lax.broadcasted_iota(jnp.int32, (rows, peers * slots), 0)
+    pack = (slot_source_ref[...] == place).astype(F32).T.astype(BF16)
 
     def send_chunk(index, carry):
         chunk = lax.rem((1 - side) * half + index, CHUNKS)
@@ -94,8 +104,26 @@
 
     lax.fori_loop(0, CHUNKS, send_chunk, 0)
 
-    slot = lax.broadcasted_iota(jnp.int32, (rows, peers * slots), 1)
-    compact = (row_slot_ref[...] == slot).astype(BF16)
+    places = jnp.broadcast_to(slot_place_ref[...].astype(F32), (128, peers * slots)).T
+    place_out[...] = places.reshape(peers, slots, 128)
+
+    def send_places(step, carry):
+        peer = lax.rem(me + step, peers)
+        pltpu.make_async_remote_copy(
+            src_ref=place_out.at[peer],
+            dst_ref=place_in.at[me],
+            send_sem=place_sem.at[0],
+            recv_sem=place_sem.at[1],
+            device_id={"col": side * peers + peer},
+            device_id_type=MESH,
+        ).start()
+        return carry
+
+    lax.fori_loop(1, peers, send_places, 0)
+    place_in[me] = place_out[me]
+
+    slot = lax.broadcasted_iota(jnp.int32, (peers * slots, rows), 0)
+    compact = (row_slot_ref[...] == slot).astype(F32).T.astype(BF16)
 
     def arrived(index):
         pltpu.make_async_copy(
@@ -117,7 +145,7 @@
         return pltpu.make_async_copy(other_buf.at[index], other_hbm.at[index], write_sem.at[index])
 
     def write_own(index):
-        source = both_buf.at[index, pl.ds(pl.multiple_of(side * rows, rows), rows)]
+        source = both_buf.at[EARLY + index, pl.ds(pl.multiple_of(side * rows, rows), rows)]
         return pltpu.make_async_copy(source, own_hbm.at[index], write_sem.at[half + index])
 
     def write_both(index):
@@ -133,13 +161,40 @@
 
     def keep_chunk(index, carry):
         both_buf[index, pl.ds(pl.multiple_of(side * rows, rows), rows)] = arrived(half + index)
+        return carry
+
+    lax.fori_loop(0, half, keep_chunk, 0)
+    for index in range(half - EARLY):
         write_own(index).start()
-        return carry
-
-    lax.fori_loop(0, half, keep_chunk, 0)
+
+    several = place_in.at[pl.ds(0, peers - 1)]
+    pltpu.make_async_copy(several, several, place_sem.at[1]).wait()
+    listed = select_rows(compact, place_in[...].reshape(peers * slots, 128)).T[:8]
+    first_row = lax.broadcasted_iota(jnp.int32, listed.shape, 0) == 0
+    note_out[...] = jnp.where(first_row, listed, send_slot_ref[0].astype(F32))
+    note_in[side] = note_out[...]
+    note_copy = pltpu.make_async_remote_copy(
+        src_ref=note_out,
+        dst_ref=note_in.at[side],
+        send_sem=note_sem.at[0],
+        recv_sem=note_sem.at[1],
+        device_id={"col": mirror},
+        device_id_type=MESH,
+    )
+    note_copy.start()
 
     gram_buf[...] = jnp.zeros_like(gram_buf)
     cross_buf[...] = jnp.zeros_like(cross_buf)
+
+    def early_copy(index):
+        return pltpu.make_async_remote_copy(
+            src_ref=both_buf.at[index, pl.ds(pl.multiple_of(side * rows, rows), rows)],
+            dst_ref=early_buf.at[index],
+            send_sem=early_sem.at[0, index],
+            recv_sem=early_sem.at[1, index],
+            device_id={"col": mirror},
+            device_id_type=MESH,
+        )
 
     def gram_chunk(index, carry):
         cross_copy(index).wait_recv()
@@ -149,25 +204,85 @@
         cross_buf[...] += cross
         return carry
 
-    lax.fori_loop(0, half, gram_chunk, 0)
+    lax.fori_loop(0, half - 1, gram_chunk, 0)
+    early_copy(0).start()
+    gram_chunk(half - 1, 0)
     gram = gram_buf[...] + cross_buf[...].T
     quarter = rows // 2
     place = 0
     for i in range(4):
         for j in range(i + 1):
-            tri_ref[place * quarter:(place + 1) * quarter, :] = gram[
+            tri_buf[place * quarter:(place + 1) * quarter, :] = gram[
                 i * quarter:(i + 1) * quarter, j * quarter:(j + 1) * quarter
             ]
             place += 1
 
+    size = parts.shape[1]
+
+    def piece(index):
+        return pl.ds(pl.multiple_of(index * size, size), size)
+
+    def part_copy(step):
+        return pltpu.make_async_remote_copy(
+            src_ref=tri_buf.at[piece(lax.rem(ring + step, count))],
+            dst_ref=parts.at[ring],
+            send_sem=sum_sem.at[0],
+            recv_sem=sum_sem.at[1],
+            device_id=ring_device(step),
+            device_id_type=MESH,
+        )
+
+    def total_copy(step):
+        return pltpu.make_async_remote_copy(
+            src_ref=total.at[ring],
+            dst_ref=total.at[ring],
+            send_sem=sum_sem.at[2],
+            recv_sem=sum_sem.at[3],
+            device_id=ring_device(step),
+            device_id_type=MESH,
+        )
+
+    for step in range(1, count):
+        part_copy(step).start()
+    early_copy(1).start()
+    parts[ring] = tri_buf[piece(ring), :]
+    pieces = parts.at[pl.ds(0, count - 1)]
+    pltpu.make_async_copy(pieces, pieces, sum_sem.at[1]).wait()
+    value = parts[0]
+    for index in range(1, count):
+        value = value + parts[index]
+    total[ring] = value
+    for step in range(1, count):
+        total_copy(step).start()
+    early_copy(2).start()
+    pltpu.make_async_copy(pieces, pieces, sum_sem.at[3]).wait()
+    tri_ref[...] = total[...].reshape(tri_ref.shape)
+    pltpu.make_async_copy(pieces, pieces, sum_sem.at[0]).wait()
+    pltpu.make_async_copy(pieces, pieces, sum_sem.at[2]).wait()
+
+    def write_early(index):
+        return pltpu.make_async_copy(early_buf.at[index], early_hbm.at[index], early_sem.at[2, index])
+
+    for index in range(EARLY):
+        early_copy(index).wait_recv()
+        write_early(index).start()
+    for index in range(EARLY):
+        early_copy(index).wait_send()
+        write_early(index).wait()
+
+    note_copy.wait()
+    note_ref[...] = note_in[...]
+    pltpu.make_async_copy(several, several, place_sem.at[0]).wait()
+
     def finish(index, carry):
         cross_copy(index).wait_send()
         write_other(index).wait()
+        write_both(index).wait()
+        return carry
+
+    lax.fori_loop(0, half, finish, 0)
+    for index in range(half - EARLY):
         write_own(index).wait()
-        write_both(index).wait()
-        return carry
-
-    lax.fori_loop(0, half, finish, 0)
 
     def sent(index, carry):
         pltpu.make_async_copy(
@@ -178,110 +293,58 @@
     lax.fori_loop(0, CHUNKS, sent, 0)
 
 
-def exchange(x, slot_source, row_slot, peers):
+def exchange(x, slot_source, slot_place, row_slot, send_slot, peers, row_count):
     rows, columns = x.shape
     width = columns // CHUNKS
     half = CHUNKS // 2
-    slots = slot_source.shape[0] // peers
+    count = 2 * row_count
+    slots = slot_source.shape[1] // peers
     any_space = pl.BlockSpec(memory_space=pl.ANY)
     vmem = pl.BlockSpec(memory_space=pltpu.VMEM)
+    smem = pl.BlockSpec(memory_space=pltpu.SMEM)
     return pl.pallas_call(
-        functools.partial(exchange_kernel, peers),
+        functools.partial(exchange_kernel, peers, row_count),
         out_shape=[
-            jax.ShapeDtypeStruct((half, rows, width), F32),
+            jax.ShapeDtypeStruct((half - EARLY, rows, width), F32),
             jax.ShapeDtypeStruct((half, rows, width), F32),
             jax.ShapeDtypeStruct((half, 2 * rows, width), F32),
+            jax.ShapeDtypeStruct((EARLY, rows, width), F32),
             jax.ShapeDtypeStruct((10 * rows // 2, rows // 2), F32),
+            jax.ShapeDtypeStruct((2, 8, rows), F32),
         ],
-        in_specs=[vmem, vmem, vmem],
-        out_specs=[any_space, any_space, any_space, vmem],
+        in_specs=[vmem, vmem, vmem, vmem, smem],
+        out_specs=[any_space, any_space, any_space, any_space, vmem, vmem],
         scratch_shapes=[
             pltpu.VMEM((CHUNKS, peers, slots, width), F32),
             pltpu.VMEM((CHUNKS, peers, slots, width), F32),
             pltpu.VMEM((half, 2 * rows, width), F32),
             pltpu.VMEM((half, rows, width), F32),
+            pltpu.VMEM((EARLY, rows, width), F32),
             pltpu.VMEM((2 * rows, 2 * rows), F32),
             pltpu.VMEM((2 * rows, 2 * rows), F32),
+            pltpu.VMEM((peers, slots, 128), F32),
+            pltpu.VMEM((peers, slots, 128), F32),
+            pltpu.VMEM((8, rows), F32),
+            pltpu.VMEM((2, 8, rows), F32),
+            pltpu.VMEM((10 * rows // 2, rows // 2), F32),
+            pltpu.VMEM((count, 5 * rows // count, rows // 2), F32),
+            pltpu.VMEM((count, 5 * rows // count, rows // 2), F32),
             pltpu.SemaphoreType.DMA((CHUNKS,)),
             pltpu.SemaphoreType.DMA((CHUNKS,)),
             pltpu.SemaphoreType.DMA((half,)),
             pltpu.SemaphoreType.DMA((half,)),
             pltpu.SemaphoreType.DMA((3 * half,)),
+            pltpu.SemaphoreType.DMA((2,)),
+            pltpu.SemaphoreType.DMA((2,)),
+            pltpu.SemaphoreType.DMA((3, EARLY)),
+            pltpu.SemaphoreType.DMA((4,)),
         ],
         compiler_params=pltpu.CompilerParams(
             collective_id=0, has_side_effects=True, vmem_limit_bytes=56 << 20
         ),
         cost_estimate=pl.CostEstimate(flops=10**10, bytes_accessed=10**8, transcendentals=0),
         name="exchange",
-    )(x, slot_source, row_slot)
-
-
-def sum_kernel(peers, row_count, tri_ref, out_ref, parts, total, out_sem, in_sem, back_out_sem, back_in_sem):
-    col = lax.axis_index("col")
-    side = col // peers
-    row = lax.axis_index("row")
-    count = 2 * row_count
-    me = side * row_count + row
-    size = parts.shape[1]
-
-    def device(index):
-        return {"col": (index // row_count) * peers + col % peers, "row": index % row_count}
-
-    barrier = pltpu.get_barrier_semaphore()
-    for step in range(1, count):
-        pl.semaphore_signal(barrier, inc=1, device_id=device(lax.rem(me + step, count)), device_id_type=MESH)
-    pl.semaphore_wait(barrier, count - 1)
-
-    def piece(index):
-        return pl.ds(pl.multiple_of(index * size, size), size)
-
-    for step in range(1, count):
-        to = lax.rem(me + step, count)
-        pltpu.make_async_remote_copy(
-            src_ref=tri_ref.at[piece(to)], dst_ref=parts.at[me], send_sem=out_sem, recv_sem=in_sem,
-            device_id=device(to), device_id_type=MESH,
-        ).start()
-    parts[me] = tri_ref[piece(me), :]
-    several = parts.at[pl.ds(0, count - 1)]
-    pltpu.make_async_copy(several, several, in_sem).wait()
-    value = parts[0]
-    for index in range(1, count):
-        value = value + parts[index]
-    total[me] = value
-    for step in range(1, count):
-        to = lax.rem(me + step, count)
-        pltpu.make_async_remote_copy(
-            src_ref=total.at[me], dst_ref=total.at[me], send_sem=back_out_sem, recv_sem=back_in_sem,
-            device_id=device(to), device_id_type=MESH,
-        ).start()
-    several = total.at[pl.ds(0, count - 1)]
-    pltpu.make_async_copy(several, several, back_in_sem).wait()
-    out_ref[...] = total[...].reshape(out_ref.shape)
-    pltpu.make_async_copy(several, several, out_sem).wait()
-    pltpu.make_async_copy(several, several, back_out_sem).wait()
-
-
-def sum_over_devices(tri, peers, row_count):
-    count = 2 * row_count
-    size = tri.shape[0] // count
-    vmem = pl.BlockSpec(memory_space=pltpu.VMEM)
-    return pl.pallas_call(
-        functools.partial(sum_kernel, peers, row_count),
-        out_shape=jax.ShapeDtypeStruct(tri.shape, F32),
-        in_specs=[vmem],
-        out_specs=vmem,
-        scratch_shapes=[
-            pltpu.VMEM((count, size, tri.shape[1]), F32),
-            pltpu.VMEM((count, size, tri.shape[1]), F32),
-            pltpu.SemaphoreType.DMA,
-            pltpu.SemaphoreType.DMA,
-            pltpu.SemaphoreType.DMA,
-            pltpu.SemaphoreType.DMA,
-        ],
-        compiler_params=pltpu.CompilerParams(collective_id=1, has_side_effects=True),
-        cost_estimate=pl.CostEstimate(flops=10**9, bytes_accessed=10**8, transcendentals=0),
-        name="sum_over_devices",
-    )(tri)
+    )(x, slot_source, slot_place, row_slot, send_slot)
 
 
 def inverse_factors(blocks):
@@ -297,16 +360,38 @@
             left = jnp.concatenate([block[8 * g:8 * g + 8, :], jnp.zeros((8, size), F32)], axis=1)
             parts.append(left + unit)
         held.append(parts)
-    for j in range(size):
+    pivots = 8
+    wide = (8, 2 * size)
+    for j in range(0, size, pivots):
         first, within = divmod(j, 8)
         for parts in held:
-            row = parts[first][within:within + 1, :]
-            scaled = row * (1.0 / row[:, j:j + 1])
+            top = [jnp.broadcast_to(parts[first][within + k:within + k + 1, :], wide) for k in range(pivots)]
+            pivot = [
+                [jnp.broadcast_to(top[k][:, j + m:j + m + 1], wide) for m in range(pivots)] for k in range(pivots)
+            ]
+            columns = [
+                [jnp.broadcast_to(parts[g][:, j + k:j + k + 1], wide) for g in range(first, groups)]
+                for k in range(pivots)
+            ]
+            scaled = []
+            for k in range(pivots):
+                inverse = 1.0 / pivot[k][k]
+                for m in range(k + 1, pivots):
+                    factor = pivot[k][m] * inverse
+                    for n in range(m, pivots):
+                        pivot[m][n] = pivot[m][n] - factor * pivot[k][n]
+                    top[m] = top[m] - factor * top[k]
+                    columns[m] = [c - factor * d for c, d in zip(columns[m], columns[k])]
+                scaled.append(top[k] * inverse)
             for g in range(first, groups):
-                column = parts[g][:, j:j + 1]
+                value = parts[g]
+                for k in range(pivots):
+                    value = value - columns[k][g - first] * scaled[k]
                 if g == first:
-                    column = jnp.where(sublane[:, :1] > within, column, 0.0)
-                parts[g] = parts[g] - column * scaled
+                    value = jnp.where(sublane >= within + pivots, value, parts[g])
+                    for k in range(pivots):
+                        value = jnp.where(sublane == within + k, top[k], value)
+                parts[g] = value
     result = []
     for parts in held:
         rows = []
@@ -348,7 +433,7 @@
     return [work[:, size:] for work in work_refs]
 
 
-def rotation_kernel(tri_ref, position_ref, own_slot_ref, partner_slot_ref, weight_ref, gram_buf, work_a, work_b):
+def rotation_kernel(tri_ref, note_ref, side_ref, weight_ref, gram_buf, work_a, work_b):
     quarter = tri_ref.shape[1]
     size = 2 * quarter
     place = 0
@@ -359,16 +444,21 @@
             if i != j:
                 gram_buf[j * quarter:(j + 1) * quarter, i * quarter:(i + 1) * quarter] = block.T
             place += 1
+    side = side_ref[0]
+    position = jnp.concatenate([note_ref[0, :1], note_ref[1, :1]], axis=1)
     slot = lax.broadcasted_iota(jnp.int32, (2 * size, 2 * size), 0)
-    place_of = (slot == position_ref[...]).astype(BF16)
+    slot = jnp.where(side == 0, slot, (slot + size) % (2 * size))
+    place_of = (slot.astype(F32) == position).astype(BF16)
+    own_slot = note_ref[side, 1:2, :1]
+    partner_slot = note_ref[1 - side, 1:2, :1]
     half_way = select_rows(place_of, gram_buf[...])
     gram_buf[...] = select_rows(place_of, half_way.T)
     own = gram_buf[:size, :size]
     partner = gram_buf[size:, size:]
     between = gram_buf[:size, size:]
     own_turn, partner_turn = orthogonal_steps([own, partner], [work_a, work_b])
-    own_part = jnp.where(own_slot_ref[0] == 0, own_turn[quarter:], own_turn[:quarter])
-    partner_part = jnp.where(partner_slot_ref[0] == 0, partner_turn[:quarter], partner_turn[quarter:])
+    own_part = jnp.where(own_slot == 0, own_turn[quarter:], own_turn[:quarter])
+    partner_part = jnp.where(partner_slot == 0, partner_turn[:quarter], partner_turn[quarter:])
     nt = ((1,), (1,))
     upper = dot_f32(dot_f32(own_part, own), own_part, nt)
     lower = dot_f32(dot_f32(partner_part, partner), partner_part, nt)
@@ -386,14 +476,14 @@
     weight_ref[...] = (dot(high, place_of) + dot(middle, place_of)) + dot(low, place_of)
 
 
-def rotations(tri, position, own_slot, partner_slot):
+def rotations(tri, note, side):
     size = 2 * tri.shape[1]
     vmem = pl.BlockSpec(memory_space=pltpu.VMEM)
     smem = pl.BlockSpec(memory_space=pltpu.SMEM)
     return pl.pallas_call(
         rotation_kernel,
         out_shape=jax.ShapeDtypeStruct((size, 2 * size), F32),
-        in_specs=[vmem, vmem, smem, smem],
+        in_specs=[vmem, vmem, smem],
         out_specs=vmem,
         scratch_shapes=[
             pltpu.VMEM((2 * size, 2 * size), F32),
@@ -403,7 +493,7 @@
         compiler_params=pltpu.CompilerParams(vmem_limit_bytes=32 << 20),
         cost_estimate=pl.CostEstimate(flops=6 * 10**10, bytes_accessed=10**8, transcendentals=0),
         name="rotations",
-    )(tri, position, own_slot, partner_slot)
+    )(tri, note, side)
 
 
 def product3(a, b):
@@ -440,15 +530,16 @@
     )(start, weight, both)
 
 
-def apply_rest_kernel(start_ref, weight_ref, own_ref, mirror_ref, partial_ref, out_ref):
+def apply_rest_kernel(start_ref, weight_ref, own_ref, early_ref, mirror_ref, partial_ref, out_ref):
     rows = own_ref.shape[1]
     side = start_ref[0]
     own_weight = jnp.where(side == 0, weight_ref[:, :rows], weight_ref[:, rows:])
     mirror_weight = jnp.where(side == 0, weight_ref[:, rows:], weight_ref[:, :rows])
-    out_ref[...] = product3(own_weight, own_ref[0]) + product3(mirror_weight, mirror_ref[0])
-
-
-def apply_rest(start, weight, own, mirror, partial):
+    crossed = jnp.where(pl.program_id(0) < EARLY, early_ref[0], mirror_ref[0])
+    out_ref[...] = product3(own_weight, own_ref[0]) + product3(mirror_weight, crossed)
+
+
+def apply_rest(start, weight, own, early, mirror, partial):
     chunks, rows, width = own.shape
     size = weight.shape[0]
     return pl.pallas_call(
@@ -459,17 +550,18 @@
             in_specs=[
                 pl.BlockSpec((size, 2 * rows), lambda i, s: (0, 0)),
                 pl.BlockSpec((1, rows, width), lambda i, s: (i, 0, 0)),
-                pl.BlockSpec((1, rows, width), lambda i, s: (i, 0, 0)),
+                pl.BlockSpec((1, rows, width), lambda i, s: (jnp.minimum(i, EARLY - 1), 0, 0)),
+                pl.BlockSpec((1, rows, width), lambda i, s: (jnp.maximum(i - EARLY, 0), 0, 0)),
                 pl.BlockSpec(memory_space=pl.ANY),
             ],
             out_specs=pl.BlockSpec((size, width), lambda i, s: (0, (1 - s[0]) * chunks + i)),
         ),
         out_shape=jax.ShapeDtypeStruct(partial.shape, F32),
-        input_output_aliases={4: 0},
+        input_output_aliases={5: 0},
         cost_estimate=pl.CostEstimate(flops=10**10, bytes_accessed=10**7, transcendentals=0),
         compiler_params=pltpu.CompilerParams(vmem_limit_bytes=32 << 20),
         name="apply_rest",
-    )(start, weight, own, mirror, partial)
+    )(start, weight, own, early, mirror, partial)
 
 
 def slot_tables(dest_ids, col, peers, slots):
@@ -482,7 +574,10 @@
     rank = jnp.sum(earlier.astype(jnp.int32), axis=1)
     wanted = jnp.arange(peers * slots, dtype=jnp.int32)
     slot = peer * slots + rank
-    slot_source = jnp.max(jnp.where(slot[None, :] == wanted[:, None], local[None, :], -1), axis=1)
+    place = target // peers * rows + dest_ids % rows
+    both = jnp.max(jnp.where(slot[None, :] == wanted[:, None], (place * rows + local)[None, :], -1), axis=1)
+    slot_source = jnp.where(both < 0, -1, both % rows)
+    slot_place = both // rows
     offset = (target - col) % peers
     amount = jnp.sum((offset[None, :] == jnp.arange(peers, dtype=jnp.int32)[:, None]).astype(jnp.int32), axis=1)
     sender = jnp.arange(peers, dtype=jnp.int32)
@@ -494,28 +589,7 @@
     within = jnp.arange(slots, dtype=jnp.int32)
     row_of_slot = jnp.where(within[None, :] < from_sender[:, None], base[:, None] + within[None, :], -1).reshape(-1)
     row_slot = jnp.max(jnp.where(row_of_slot[None, :] == local[:, None], wanted[None, :], -1), axis=1)
-    return slot_source[:, None], row_slot[:, None]
-
-
-def final_positions(every_id, col, peers, slots):
-    devices, rows = every_id.shape
-    target = every_id // rows
-    mine = target % peers == col % peers
-    place = jnp.where(target == col, 0, rows) + every_id % rows
-    local = jnp.arange(rows, dtype=jnp.int32)
-    before = (local[:, None] < local[None, :]).astype(BF16)
-    rank = jnp.dot(mine.astype(BF16), before, preferred_element_type=F32).astype(jnp.int32)
-    within = jnp.arange(slots, dtype=jnp.int32)
-    held = jnp.max(
-        jnp.where(mine[:, None, :] & (rank[:, None, :] == within[None, :, None]), place[:, None, :], -1), axis=2
-    )
-    amount = jnp.sum(mine.astype(jnp.int32), axis=1)
-    device = jnp.arange(devices, dtype=jnp.int32)
-    base = jnp.sum(jnp.where(device[None, :] < device[:, None], amount[None, :], 0), axis=1)
-    row_of = jnp.where(held >= 0, base[:, None] + within[None, :], -1).reshape(-1)
-    wanted = jnp.arange(2 * rows, dtype=jnp.int32)
-    position = jnp.max(jnp.where(row_of[:, None] == wanted[None, :], held.reshape(-1)[:, None], -1), axis=0)
-    return position[None, :]
+    return slot_source[None, :], slot_place[None, :], row_slot[None, :]
 
 
 def body(row_count, greens_matrix, dest_ids, send_slot):
@@ -525,19 +599,15 @@
     cap = max(2, 2 * rows // count)
     slots = 2 * cap
     col = lax.axis_index("col")
-    every_id = lax.all_gather(dest_ids, "col")
-    every_slot = lax.all_gather(send_slot, "col").reshape(-1)
-    slot_source, row_slot = slot_tables(dest_ids, col, peers, slots)
-    own, other, both, tri = exchange(greens_matrix, slot_source, row_slot, peers)
+    side = (col // peers).astype(jnp.int32)[None]
+    slot_source, slot_place, row_slot = slot_tables(dest_ids, col, peers, slots)
+    own, other, both, early, tri, note = exchange(
+        greens_matrix, slot_source, slot_place, row_slot, send_slot, peers, row_count
+    )
     mirror = lax.ppermute(own, "col", [(i, i ^ peers) for i in range(count)])
-    tri = sum_over_devices(tri, peers, row_count)
-    position = final_positions(every_id, col, peers, slots)
-    device = jnp.arange(count, dtype=jnp.int32)
-    partner_slot = jnp.sum(jnp.where(device == (col + peers) % count, every_slot, 0))[None]
-    weight = rotations(tri, position, send_slot, partner_slot)
-    side = (col // peers).astype(jnp.int32)[None]
+    weight = rotations(tri, note, side)
     partial = apply_both(side, weight, both, columns)
-    return apply_rest(side, weight, other, mirror, partial)
+    return apply_rest(side, weight, other, early, mirror, partial)
 
 
 def solution(mesh):

time: 504 us -> 264 us (0.52)
  the two profiles are of different devices: /device:TPU:94 before, /device:TPU:1 now
where the time goes in v2:
time: 264 us; the launch traced here: 260 us
  Pallas kernels  249 us (94%)
  starting transfers between devices  4.3 us (2%)
  other arithmetic  3.58 us (1%)
    pallas_call x1, Pallas kernels, exchange(): pl.pallas_call(functools.partial(exchange_kernel, peers, row_count), out_...  186 us
    pallas_call x1, Pallas kernels, rotations(): pl.pallas_call(rotation_kernel, out_shape=jax.ShapeDtypeStruct((size, 2 *...  53.7 us
  transfers between devices with their start and end apart: 1, of which 0 were waited for; matrix products, arithmetic and copies ran while one was open for 0% of the time, Pallas kernels for 23%

profile of v2, /device:TPU:1, one launch (start us, length us, event | category | flops | bytes accessed | tf_op | source)
XLA Modules:
  0.0 260.1 jit_solution(3867755196244750970)
XLA Ops:
  0.7 0.7 and_select_fusion.2
  1.4 0.1 convert_reduce_fusion.1
  1.5 0.2 select_reduce_fusion.3
  1.7 0.1 select_reduce_fusion.2
  1.8 0.7 and_select_fusion.6
  2.5 0.2 convert_reduce_fusion
  2.7 0.2 select_reduce_fusion.1
  2.8 0.6 and_select_fusion
  3.5 0.1 add_select_fusion
  3.5 0.1 select_n.113
  3.6 0.7 select_reduce_fusion
  4.3 185.8 %exchange.1 = (f32[5,256,256]{2,1,0:T(8,128)}, f32[8,256,256]{2,1,0:T(8,128)}, f32[8,512,256]{2,1,0:T(8,128)}, f32[3,256,256]{2,1,0:T(8,128)}, f32[1280,128]{1,0:T(8,128)}, /*index=5*/f32[2,8,256]{2,1,0:T(8,128)}) custom-call(f32[256,4096]{1,0:T(8,128)} %x_ref.1, s32[1,512]{1,0:T(1,128)} %get-tuple-element.20.slot_source_ref, ...), custom_call_target="tpu_custom_call" | custom-call | flops 10000000000 | bytes 100000000 | tf_op jit(solution)/shard_map/exchange/pallas_call | solution.py:305
  190.1 4.3 %collective-permute-start = (f32[5,256,256]{2,1,0:T(8,128)}, f32[5,256,256]{2,1,0:T(8,128)S(1)}, u32[]{:S(2)}, u32[]{:S(2)}) collective-permute-start(f32[5,256,256]{2,1,0:T(8,128)} %get-tuple-element.15), channel_id=1, source_target_pairs={{0,128},{4,132},{8,136},{12,140},{16,144},{20,148},{24,152},{28,15... | collective-permute-start | bytes 3932168 | tf_op jit(solution)/shard_map/ppermute | solution.py:607
  194.4 0.0 copy-start.3
  194.4 1.1 copy-done.3
  195.5 0.0 copy-start.4
  195.5 0.7 copy-done.4
  196.2 0.0 copy-start
  196.2 53.7 %rotations.1.weight_ref = f32[256,512]{1,0:T(8,128)S(1)} custom-call(f32[1280,128]{1,0:T(8,128)S(1)} %copy-done.3, f32[2,8,256]{2,1,0:T(8,128)S(1)} %copy-done.4, s32[1]{0:T(128)} %bitcast.side_ref.start_ref), custom_call_target="tpu_custom_call" | custom-call | flops 60000002048 | bytes 100000000 | tf_op jit(solution)/shard_map/rotations/pallas_call | solution.py:483
  249.9 0.0 copy-done
  250.0 0.0 copy-start.1
  250.0 0.0 copy-start.2
  250.0 4.9 %apply_both.1.partial_ref = f32[256,4096]{1,0:T(8,128)} custom-call(s32[1]{0:T(128)} %bitcast.side_ref.start_ref, f32[256,512]{1,0:T(8,128)S(1)} %rotations.1.weight_ref, f32[8,512,256]{2,1,0:T(8,128)S(1)} %copy-done), custom_call_target="tpu_custom_call" | custom-call | flops 10000000000 | bytes 10000000 | tf_op jit(solution)/shard_map/apply_both/pallas_call | solution.py:515
  254.8 0.0 collective-permute-done.mirror_ref
  254.8 0.0 copy-done.1
  254.8 0.0 copy-done.2
  254.8 5.0 %apply_rest.1 = f32[256,4096]{1,0:T(8,128)} custom-call(s32[1]{0:T(128)} %bitcast.side_ref.start_ref, f32[256,512]{1,0:T(8,128)S(1)} %rotations.1.weight_ref, f32[8,256,256]{2,1,0:T(8,128)S(1)} %copy-done.1, f32[3,256,256]{2,1,0:T(8,128)S(1)} %copy-done.2, f32[5,256,256]{2,1,0:T(8,128)S(1)} %collective-permute-done.mirror_ref, ...), custom_call_target="tpu_custom_call", output_to_operand_aliasing={{}: (5, {})} | custom-call | flops 10000000000 | bytes 10000000 | tf_op jit(solution)/shard_map/apply_rest/pallas_call | solution.py:545
  (2 shorter events, 0.0 us)
Async XLA Ops:
  190.1 64.7 %collective-permute-start = (f32[5,256,256]{2,1,0:T(8,128)}, f32[5,256,256]{2,1,0:T(8,128)S(1)}, u32[]{:S(2)}, u32[]{:S(2)}) collective-permute-start(f32[5,256,256]{2,1,0:T(8,128)} %get-tuple-element.15), channel_id=1, source_target_pairs={{0,128},{4,132},{8,136},{12,140},{16,144},{20,148},{24,152},{28,15... | collective-permute-start | bytes 3932168 | tf_op jit(solution)/shard_map/ppermute | solution.py:607
  194.4 1.1 copy-start.3
  195.5 0.7 copy-start.4
  196.2 53.7 %copy-start = (f32[8,512,256]{2,1,0:T(8,128)S(1)}, f32[8,512,256]{2,1,0:T(8,128)}, u32[]{:S(2)}) copy-start(f32[8,512,256]{2,1,0:T(8,128)} %get-tuple-element.16.both_ref) | copy-start | bytes 12582916
  250.0 4.9 %copy-start.1 = (f32[8,256,256]{2,1,0:T(8,128)S(1)}, f32[8,256,256]{2,1,0:T(8,128)}, u32[]{:S(2)}) copy-start(f32[8,256,256]{2,1,0:T(8,128)} %get-tuple-element.13.own_ref) | copy-start | bytes 6291460
  250.0 4.9 %copy-start.2 = (f32[3,256,256]{2,1,0:T(8,128)S(1)}, f32[3,256,256]{2,1,0:T(8,128)}, u32[]{:S(2)}) copy-start(f32[3,256,256]{2,1,0:T(8,128)} %get-tuple-element.14.early_ref) | copy-start | bytes 2359300

commit v3 on v2

--- a/solution.py
+++ b/solution.py
@@ -8,7 +8,8 @@
 from jax.sharding import PartitionSpec as P
 
 CHUNKS = 16
-EARLY = 3
+EARLY = 2
+TOGETHER = 2
 BLOCK = 64
 F32 = jnp.float32
 BF16 = jnp.bfloat16
@@ -43,11 +44,11 @@
 
 
 def exchange_kernel(
-    peers, row_count, x_ref, slot_source_ref, slot_place_ref, row_slot_ref, send_slot_ref,
+    peers, row_count, x_hbm, row_slot_ref, row_place_ref, slot_row_ref, send_slot_ref,
     own_hbm, other_hbm, both_hbm, early_hbm, tri_ref, note_ref,
-    out_buf, in_buf, both_buf, other_buf, early_buf, gram_buf, cross_buf, place_out, place_in, note_out, note_in,
+    x_buf, out_buf, in_buf, both_buf, other_buf, early_buf, gram_buf, cross_buf, place_out, place_in, note_out, note_in,
     tri_buf, parts, total,
-    out_sem, in_sem, z_out_sem, z_in_sem, write_sem, place_sem, note_sem, early_sem, sum_sem,
+    x_sem, out_sem, in_sem, z_out_sem, z_in_sem, write_sem, place_sem, note_sem, early_sem, sum_sem,
 ):
     col = lax.axis_index("col")
     side = col // peers
@@ -58,6 +59,16 @@
     width = out_buf.shape[3]
     rows = other_buf.shape[1]
 
+    def read_chunk(index):
+        chunk = lax.rem((1 - side) * half + index, CHUNKS)
+        piece = x_hbm.at[:, pl.ds(pl.multiple_of(chunk * width, width), width)]
+        return pltpu.make_async_copy(piece, x_buf.at[index], x_sem.at[index])
+
+    def start_read(index, carry):
+        read_chunk(index).start()
+        return carry
+
+    lax.fori_loop(0, CHUNKS, start_read, 0)
     barrier = pltpu.get_barrier_semaphore()
 
     def greet(step, carry):
@@ -77,14 +88,12 @@
         pl.semaphore_signal(barrier, inc=1, device_id=ring_device(step), device_id_type=MESH)
     pl.semaphore_wait(barrier, peers - 1 + count - 1)
 
-    place = lax.broadcasted_iota(jnp.int32, (rows, peers * slots), 0)
-    pack = (slot_source_ref[...] == place).astype(F32).T.astype(BF16)
+    slot = lax.broadcasted_iota(jnp.int32, (peers * slots, rows), 0)
+    pack = (row_slot_ref[...] == slot).astype(BF16)
 
     def send_chunk(index, carry):
-        chunk = lax.rem((1 - side) * half + index, CHUNKS)
-        piece = x_ref[:, pl.ds(pl.multiple_of(chunk * width, width), width)]
-        packed = select_rows(pack, piece).reshape(peers, slots, width)
-        out_buf[index] = packed
+        read_chunk(index).wait()
+        out_buf[index] = select_rows(pack, x_buf[index]).reshape(peers, slots, width)
 
         def send(step, inner):
             peer = lax.rem(me + step, peers)
@@ -104,8 +113,8 @@
 
     lax.fori_loop(0, CHUNKS, send_chunk, 0)
 
-    places = jnp.broadcast_to(slot_place_ref[...].astype(F32), (128, peers * slots)).T
-    place_out[...] = places.reshape(peers, slots, 128)
+    places = jnp.broadcast_to(row_place_ref[...].astype(F32), (128, rows)).T
+    place_out[...] = select_rows(pack, places).reshape(peers, slots, 128)
 
     def send_places(step, carry):
         peer = lax.rem(me + step, peers)
@@ -122,8 +131,8 @@
     lax.fori_loop(1, peers, send_places, 0)
     place_in[me] = place_out[me]
 
-    slot = lax.broadcasted_iota(jnp.int32, (peers * slots, rows), 0)
-    compact = (row_slot_ref[...] == slot).astype(F32).T.astype(BF16)
+    place = lax.broadcasted_iota(jnp.int32, (rows, peers * slots), 0)
+    compact = (slot_row_ref[...] == place).astype(BF16)
 
     def arrived(index):
         pltpu.make_async_copy(
@@ -254,7 +263,6 @@
     total[ring] = value
     for step in range(1, count):
         total_copy(step).start()
-    early_copy(2).start()
     pltpu.make_async_copy(pieces, pieces, sum_sem.at[3]).wait()
     tri_ref[...] = total[...].reshape(tri_ref.shape)
     pltpu.make_async_copy(pieces, pieces, sum_sem.at[0]).wait()
@@ -293,12 +301,12 @@
     lax.fori_loop(0, CHUNKS, sent, 0)
 
 
-def exchange(x, slot_source, slot_place, row_slot, send_slot, peers, row_count):
+def exchange(x, row_slot, row_place, slot_row, send_slot, peers, row_count):
     rows, columns = x.shape
     width = columns // CHUNKS
     half = CHUNKS // 2
     count = 2 * row_count
-    slots = slot_source.shape[1] // peers
+    slots = slot_row.shape[1] // peers
     any_space = pl.BlockSpec(memory_space=pl.ANY)
     vmem = pl.BlockSpec(memory_space=pltpu.VMEM)
     smem = pl.BlockSpec(memory_space=pltpu.SMEM)
@@ -312,9 +320,10 @@
             jax.ShapeDtypeStruct((10 * rows // 2, rows // 2), F32),
             jax.ShapeDtypeStruct((2, 8, rows), F32),
         ],
-        in_specs=[vmem, vmem, vmem, vmem, smem],
+        in_specs=[any_space, vmem, vmem, vmem, smem],
         out_specs=[any_space, any_space, any_space, any_space, vmem, vmem],
         scratch_shapes=[
+            pltpu.VMEM((CHUNKS, rows, width), F32),
             pltpu.VMEM((CHUNKS, peers, slots, width), F32),
             pltpu.VMEM((CHUNKS, peers, slots, width), F32),
             pltpu.VMEM((half, 2 * rows, width), F32),
@@ -331,6 +340,7 @@
             pltpu.VMEM((count, 5 * rows // count, rows // 2), F32),
             pltpu.SemaphoreType.DMA((CHUNKS,)),
             pltpu.SemaphoreType.DMA((CHUNKS,)),
+            pltpu.SemaphoreType.DMA((CHUNKS,)),
             pltpu.SemaphoreType.DMA((half,)),
             pltpu.SemaphoreType.DMA((half,)),
             pltpu.SemaphoreType.DMA((3 * half,)),
@@ -344,7 +354,7 @@
         ),
         cost_estimate=pl.CostEstimate(flops=10**10, bytes_accessed=10**8, transcendentals=0),
         name="exchange",
-    )(x, slot_source, slot_place, row_slot, send_slot)
+    )(x, row_slot, row_place, slot_row, send_slot)
 
 
 def inverse_factors(blocks):
@@ -433,7 +443,7 @@
     return [work[:, size:] for work in work_refs]
 
 
-def rotation_kernel(tri_ref, note_ref, side_ref, weight_ref, gram_buf, work_a, work_b):
+def rotation_kernel(tri_ref, note_ref, side_ref, high_ref, low_ref, gram_buf, work_a, work_b):
     quarter = tri_ref.shape[1]
     size = 2 * quarter
     place = 0
@@ -473,7 +483,10 @@
     gram_buf[:size, size:] = dot_f32(last[:, quarter:], partner_part)
     high, middle, low = split3(gram_buf[:size, :])
     dot = functools.partial(jnp.dot, preferred_element_type=F32)
-    weight_ref[...] = (dot(high, place_of) + dot(middle, place_of)) + dot(low, place_of)
+    weight = (dot(high, place_of) + dot(middle, place_of)) + dot(low, place_of)
+    high = weight.astype(BF16)
+    high_ref[...] = high
+    low_ref[...] = (weight - high.astype(F32)).astype(BF16)
 
 
 def rotations(tri, note, side):
@@ -482,9 +495,9 @@
     smem = pl.BlockSpec(memory_space=pltpu.SMEM)
     return pl.pallas_call(
         rotation_kernel,
-        out_shape=jax.ShapeDtypeStruct((size, 2 * size), F32),
+        out_shape=[jax.ShapeDtypeStruct((size, 2 * size), BF16)] * 2,
         in_specs=[vmem, vmem, smem],
-        out_specs=vmem,
+        out_specs=[vmem, vmem],
         scratch_shapes=[
             pltpu.VMEM((2 * size, 2 * size), F32),
             pltpu.VMEM((size, 2 * size), F32),
@@ -496,72 +509,82 @@
     )(tri, note, side)
 
 
-def product3(a, b):
-    a_high = a.astype(BF16)
-    a_low = (a - a_high.astype(F32)).astype(BF16)
+def product3(a_high, a_low, b):
     b_high = b.astype(BF16)
     b_low = (b - b_high.astype(F32)).astype(BF16)
     dot = functools.partial(jnp.dot, preferred_element_type=F32)
     return dot(a_high, b_high) + (dot(a_high, b_low) + dot(a_low, b_high))
 
 
-def apply_both_kernel(start_ref, weight_ref, both_ref, out_ref):
-    out_ref[...] = product3(weight_ref[...], both_ref[0])
-
-
-def apply_both(start, weight, both, columns):
+def apply_both_kernel(side_ref, high_ref, low_ref, both_ref, out_ref):
+    width = both_ref.shape[2]
+    for k in range(TOGETHER):
+        out_ref[:, k * width:(k + 1) * width] = product3(high_ref[...], low_ref[...], both_ref[k])
+
+
+def apply_both(side, high, low, both, columns):
     chunks, rows, width = both.shape
-    size = weight.shape[0]
+    size = high.shape[0]
+    steps = chunks // TOGETHER
+    weight = pl.BlockSpec((size, rows), lambda i, s: (0, 0))
     return pl.pallas_call(
         apply_both_kernel,
         grid_spec=pltpu.PrefetchScalarGridSpec(
             num_scalar_prefetch=1,
-            grid=(chunks,),
-            in_specs=[
-                pl.BlockSpec((size, rows), lambda i, s: (0, 0)),
-                pl.BlockSpec((1, rows, width), lambda i, s: (i, 0, 0)),
-            ],
-            out_specs=pl.BlockSpec((size, width), lambda i, s: (0, s[0] * chunks + i)),
+            grid=(steps,),
+            in_specs=[weight, weight, pl.BlockSpec((TOGETHER, rows, width), lambda i, s: (i, 0, 0))],
+            out_specs=pl.BlockSpec((size, TOGETHER * width), lambda i, s: (0, s[0] * steps + i)),
         ),
         out_shape=jax.ShapeDtypeStruct((size, columns), F32),
         cost_estimate=pl.CostEstimate(flops=10**10, bytes_accessed=10**7, transcendentals=0),
         compiler_params=pltpu.CompilerParams(vmem_limit_bytes=32 << 20),
         name="apply_both",
-    )(start, weight, both)
-
-
-def apply_rest_kernel(start_ref, weight_ref, own_ref, early_ref, mirror_ref, partial_ref, out_ref):
-    rows = own_ref.shape[1]
-    side = start_ref[0]
-    own_weight = jnp.where(side == 0, weight_ref[:, :rows], weight_ref[:, rows:])
-    mirror_weight = jnp.where(side == 0, weight_ref[:, rows:], weight_ref[:, :rows])
-    crossed = jnp.where(pl.program_id(0) < EARLY, early_ref[0], mirror_ref[0])
-    out_ref[...] = product3(own_weight, own_ref[0]) + product3(mirror_weight, crossed)
-
-
-def apply_rest(start, weight, own, early, mirror, partial):
+    )(side, high, low, both)
+
+
+def apply_rest_kernel(
+    side_ref, high_ref, low_ref, mirror_high_ref, mirror_low_ref, own_ref, early_ref, mirror_ref, partial_ref, out_ref
+):
+    width = own_ref.shape[2]
+    first = pl.program_id(0) == 0
+    for k in range(TOGETHER):
+        crossed = mirror_ref[k]
+        if k < EARLY:
+            crossed = jnp.where(first, early_ref[k], crossed)
+        out_ref[:, k * width:(k + 1) * width] = product3(high_ref[...], low_ref[...], own_ref[k]) + product3(
+            mirror_high_ref[...], mirror_low_ref[...], crossed
+        )
+
+
+def apply_rest(side, high, low, own, early, mirror, partial):
     chunks, rows, width = own.shape
-    size = weight.shape[0]
+    size = high.shape[0]
+    steps = chunks // TOGETHER
+    weight = pl.BlockSpec((size, rows), lambda i, s: (0, s[0]))
+    mirror_weight = pl.BlockSpec((size, rows), lambda i, s: (0, 1 - s[0]))
     return pl.pallas_call(
         apply_rest_kernel,
         grid_spec=pltpu.PrefetchScalarGridSpec(
             num_scalar_prefetch=1,
-            grid=(chunks,),
+            grid=(steps,),
             in_specs=[
-                pl.BlockSpec((size, 2 * rows), lambda i, s: (0, 0)),
-                pl.BlockSpec((1, rows, width), lambda i, s: (i, 0, 0)),
-                pl.BlockSpec((1, rows, width), lambda i, s: (jnp.minimum(i, EARLY - 1), 0, 0)),
-                pl.BlockSpec((1, rows, width), lambda i, s: (jnp.maximum(i - EARLY, 0), 0, 0)),
+                weight,
+                weight,
+                mirror_weight,
+                mirror_weight,
+                pl.BlockSpec((TOGETHER, rows, width), lambda i, s: (i, 0, 0)),
+                pl.BlockSpec((EARLY, rows, width), lambda i, s: (0, 0, 0)),
+                pl.BlockSpec((TOGETHER, rows, width), lambda i, s: (jnp.maximum(i - 1, 0), 0, 0)),
                 pl.BlockSpec(memory_space=pl.ANY),
             ],
-            out_specs=pl.BlockSpec((size, width), lambda i, s: (0, (1 - s[0]) * chunks + i)),
+            out_specs=pl.BlockSpec((size, TOGETHER * width), lambda i, s: (0, (1 - s[0]) * steps + i)),
         ),
         out_shape=jax.ShapeDtypeStruct(partial.shape, F32),
-        input_output_aliases={5: 0},
+        input_output_aliases={8: 0},
         cost_estimate=pl.CostEstimate(flops=10**10, bytes_accessed=10**7, transcendentals=0),
         compiler_params=pltpu.CompilerParams(vmem_limit_bytes=32 << 20),
         name="apply_rest",
-    )(start, weight, own, early, mirror, partial)
+    )(side, high, low, high, low, own, early, mirror, partial)
 
 
 def slot_tables(dest_ids, col, peers, slots):
@@ -572,12 +595,8 @@
     peer = target % peers
     earlier = (peer[:, None] == peer[None, :]) & (local[None, :] < local[:, None])
     rank = jnp.sum(earlier.astype(jnp.int32), axis=1)
-    wanted = jnp.arange(peers * slots, dtype=jnp.int32)
-    slot = peer * slots + rank
-    place = target // peers * rows + dest_ids % rows
-    both = jnp.max(jnp.where(slot[None, :] == wanted[:, None], (place * rows + local)[None, :], -1), axis=1)
-    slot_source = jnp.where(both < 0, -1, both % rows)
-    slot_place = both // rows
+    row_slot = peer * slots + rank
+    row_place = target // peers * rows + dest_ids % rows
     offset = (target - col) % peers
     amount = jnp.sum((offset[None, :] == jnp.arange(peers, dtype=jnp.int32)[:, None]).astype(jnp.int32), axis=1)
     sender = jnp.arange(peers, dtype=jnp.int32)
@@ -587,9 +606,8 @@
     )
     base = jnp.sum(jnp.where(sender[None, :] < sender[:, None], from_sender[None, :], 0), axis=1)
     within = jnp.arange(slots, dtype=jnp.int32)
-    row_of_slot = jnp.where(within[None, :] < from_sender[:, None], base[:, None] + within[None, :], -1).reshape(-1)
-    row_slot = jnp.max(jnp.where(row_of_slot[None, :] == local[:, None], wanted[None, :], -1), axis=1)
-    return slot_source[None, :], slot_place[None, :], row_slot[None, :]
+    slot_row = jnp.where(within[None, :] < from_sender[:, None], base[:, None] + within[None, :], -1).reshape(-1)
+    return row_slot[None, :], row_place[None, :], slot_row[None, :]
 
 
 def body(row_count, greens_matrix, dest_ids, send_slot):
@@ -600,14 +618,14 @@
     slots = 2 * cap
     col = lax.axis_index("col")
     side = (col // peers).astype(jnp.int32)[None]
-    slot_source, slot_place, row_slot = slot_tables(dest_ids, col, peers, slots)
+    row_slot, row_place, slot_row = slot_tables(dest_ids, col, peers, slots)
     own, other, both, early, tri, note = exchange(
-        greens_matrix, slot_source, slot_place, row_slot, send_slot, peers, row_count
+        greens_matrix, row_slot, row_place, slot_row, send_slot, peers, row_count
     )
     mirror = lax.ppermute(own, "col", [(i, i ^ peers) for i in range(count)])
-    weight = rotations(tri, note, side)
-    partial = apply_both(side, weight, both, columns)
-    return apply_rest(side, weight, other, early, mirror, partial)
+    high, low = rotations(tri, note, side)
+    partial = apply_both(side, high, low, both, columns)
+    return apply_rest(side, high, low, other, early, mirror, partial)
 
 
 def solution(mesh):

time: 264 us -> 261 us (0.989)
  Pallas kernels: 249 us -> 235 us
  waiting for transfers between devices: 0.01 us -> 11.4 us
    pallas_call x1, Pallas kernels: 186 us -> 174 us  [exchange(): pl.pallas_call(functools.partial(exchange_kernel, peers, row_count), out_...]
    ppermute x1, waiting for transfers between devices: 0.01 us -> 11.4 us  [body(): mirror = lax.ppermute(own, 'col', [(i, i ^ peers) for i in range(count)])]
  transfers between devices with their start and end apart: 1 -> 1, of which waited for: 0 -> 1; matrix products, arithmetic and copies ran while one was open for 0% -> 0% of each run, Pallas kernels for 23% -> 22%
where the time goes in v3:
time: 261 us; the launch traced here: 257 us
  Pallas kernels  235 us (90%)
  waiting for transfers between devices  11.4 us (4%)
  starting transfers between devices  3.87 us (1%)
  other arithmetic  3.23 us (1%)
    pallas_call x1, Pallas kernels, exchange(): pl.pallas_call(functools.partial(exchange_kernel, peers, row_count), out_...  174 us
    pallas_call x1, Pallas kernels, rotations(): pl.pallas_call(rotation_kernel, out_shape=[jax.ShapeDtypeStruct((size, 2...  54 us
    ppermute x1, waiting for transfers between devices, body(): mirror = lax.ppermute(own, 'col', [(i, i ^ peers) for i in range(count)])  11.4 us
  transfers between devices with their start and end apart: 1, of which 1 were waited for; matrix products, arithmetic and copies ran while one was open for 0% of the time, Pallas kernels for 22%

profile of v3, /device:TPU:1, one launch (start us, length us, event | category | flops | bytes accessed | tf_op | source)
XLA Modules:
  0.0 256.6 jit_solution(16627854358431876999)
XLA Ops:
  0.7 0.7 and_select_fusion
  1.4 0.1 convert_reduce_fusion.1
  1.5 0.2 select_reduce_fusion.1
  1.7 0.1 select_reduce_fusion
  1.8 1.3 fusion.1
  3.1 0.2 convert_reduce_fusion
  3.2 0.6 multiply_add_fusion
  3.8 0.1 add_select_fusion
  3.9 0.7 select_n.68.slot_row_ref
  4.6 173.7 %exchange.1 = (f32[6,256,256]{2,1,0:T(8,128)}, f32[8,256,256]{2,1,0:T(8,128)}, f32[8,512,256]{2,1,0:T(8,128)}, f32[2,256,256]{2,1,0:T(8,128)}, f32[1280,128]{1,0:T(8,128)}, /*index=5*/f32[2,8,256]{2,1,0:T(8,128)}) custom-call(f32[256,4096]{1,0:T(8,128)} %x_hbm.1, s32[1,256]{1,0:T(1,128)} %bitcast.3, s32[1,256]{1,0:T(1,128)} %bitcast.4, ...), custom_call_target="tpu_custom_call" | custom-call | flops 10000000000 | bytes 100000000 | tf_op jit(solution)/shard_map/exchange/pallas_call | solution.py:313
  178.3 3.9 %collective-permute-start = (f32[6,256,256]{2,1,0:T(8,128)}, f32[6,256,256]{2,1,0:T(8,128)S(1)}, u32[]{:S(2)}, u32[]{:S(2)}) collective-permute-start(f32[6,256,256]{2,1,0:T(8,128)} %get-tuple-element.19), channel_id=1, source_target_pairs={{0,128},{4,132},{8,136},{12,140},{16,144},{20,148},{24,152},{28,15... | collective-permute-start | bytes 4718600 | tf_op jit(solution)/shard_map/ppermute | solution.py:625
  182.1 0.0 copy-start.3
  182.1 1.1 copy-done.3
  183.2 0.0 copy-start.4
  183.2 0.7 copy-done.4
  183.9 0.0 copy-start
  183.9 54.0 %rotations.1 = (bf16[256,512]{1,0:T(8,128)(2,1)S(1)}, bf16[256,512]{1,0:T(8,128)(2,1)S(1)}) custom-call(f32[1280,128]{1,0:T(8,128)S(1)} %copy-done.3, f32[2,8,256]{2,1,0:T(8,128)S(1)} %copy-done.4, s32[1]{0:T(128)} %bitcast.side_ref), custom_call_target="tpu_custom_call" | custom-call | flops 60000002048 | bytes 100000000 | tf_op jit(solution)/shard_map/rotations/pallas_call | solution.py:496
  237.9 0.0 copy-done
  237.9 0.0 copy-start.1
  237.9 0.0 copy-start.2
  238.0 3.5 %apply_both.1.partial_ref = f32[256,4096]{1,0:T(8,128)} custom-call(s32[1]{0:T(128)} %bitcast.side_ref, bf16[256,512]{1,0:T(8,128)(2,1)S(1)} %get-tuple-element.15.high_ref.mirror_high_ref, bf16[256,512]{1,0:T(8,128)(2,1)S(1)} %get-tuple-element.16.low_ref.mirror_low_ref, f32[8,512,256]{2,1,0:T(8,128)S(1)} %copy-done), custom_call_target="tpu_custom_call" | custom-call | flops 10000000000 | bytes 10000000 | tf_op jit(solution)/shard_map/apply_both/pallas_call | solution.py:530
  241.4 11.4 %collective-permute-done.mirror_ref = f32[6,256,256]{2,1,0:T(8,128)S(1)} collective-permute-done((f32[6,256,256]{2,1,0:T(8,128)}, f32[6,256,256]{2,1,0:T(8,128)S(1)}, u32[]{:S(2)}, u32[]{:S(2)}) %collective-permute-start) | collective-permute-done | bytes 1572896 | tf_op jit(solution)/shard_map/ppermute | solution.py:625
  252.8 0.0 copy-done.1
  252.8 0.0 copy-done.2
  252.8 3.5 %apply_rest.1 = f32[256,4096]{1,0:T(8,128)} custom-call(s32[1]{0:T(128)} %bitcast.side_ref, bf16[256,512]{1,0:T(8,128)(2,1)S(1)} %get-tuple-element.15.high_ref.mirror_high_ref, bf16[256,512]{1,0:T(8,128)(2,1)S(1)} %get-tuple-element.16.low_ref.mirror_low_ref, ...), custom_call_target="tpu_custom_call", output_to_operand_aliasing={{}: (8, {})} | custom-call | flops 10000000000 | bytes 10000000 | tf_op jit(solution)/shard_map/apply_rest/pallas_call | solution.py:565
  (1 shorter events, 0.0 us)
Async XLA Ops:
  178.3 74.6 %collective-permute-start = (f32[6,256,256]{2,1,0:T(8,128)}, f32[6,256,256]{2,1,0:T(8,128)S(1)}, u32[]{:S(2)}, u32[]{:S(2)}) collective-permute-start(f32[6,256,256]{2,1,0:T(8,128)} %get-tuple-element.19), channel_id=1, source_target_pairs={{0,128},{4,132},{8,136},{12,140},{16,144},{20,148},{24,152},{28,15... | collective-permute-start | bytes 4718600 | tf_op jit(solution)/shard_map/ppermute | solution.py:625
  182.1 1.1 copy-start.3
  183.2 0.7 copy-start.4
  183.9 54.0 %copy-start = (f32[8,512,256]{2,1,0:T(8,128)S(1)}, f32[8,512,256]{2,1,0:T(8,128)}, u32[]{:S(2)}) copy-start(f32[8,512,256]{2,1,0:T(8,128)} %get-tuple-element.20.both_ref) | copy-start | bytes 12582916
  237.9 14.9 %copy-start.1 = (f32[8,256,256]{2,1,0:T(8,128)S(1)}, f32[8,256,256]{2,1,0:T(8,128)}, u32[]{:S(2)}) copy-start(f32[8,256,256]{2,1,0:T(8,128)} %get-tuple-element.17.own_ref) | copy-start | bytes 6291460
  237.9 14.9 %copy-start.2 = (f32[2,256,256]{2,1,0:T(8,128)S(1)}, f32[2,256,256]{2,1,0:T(8,128)}, u32[]{:S(2)}) copy-start(f32[2,256,256]{2,1,0:T(8,128)} %get-tuple-element.18.early_ref) | copy-start | bytes 1572868

commit v4 on v3

--- a/solution.py
+++ b/solution.py
@@ -10,6 +10,7 @@
 CHUNKS = 16
 EARLY = 2
 TOGETHER = 2
+LEAD = 3
 BLOCK = 64
 F32 = jnp.float32
 BF16 = jnp.bfloat16
@@ -43,8 +44,37 @@
     return dot(high, high) + dot(middle, middle) + cross, cross
 
 
+def slot_tables(ids, col, peers, slots):
+    rows = ids.shape[1]
+
+    def log2(number):
+        return number.bit_length() - 1
+
+    def upright(values):
+        return jnp.broadcast_to(values, (128, rows)).T[:, :1]
+
+    target = lax.shift_right_logical(ids, log2(rows))
+    peer = target & (peers - 1)
+    row_place = (lax.shift_right_logical(target, log2(peers)) * rows + (ids & (rows - 1))).astype(F32)
+    sender = upright(((col - ((target - col) & (peers - 1))) & (peers - 1)).astype(F32))
+    peer = peer.astype(F32)
+    earlier = lax.broadcasted_iota(jnp.int32, (rows, rows), 0) < lax.broadcasted_iota(jnp.int32, (rows, rows), 1)
+    same = jnp.where(upright(peer) == peer, 1.0, 0.0)
+    rank = jnp.sum(jnp.where(earlier, same, 0.0), axis=0, keepdims=True)
+    slot = lax.broadcasted_iota(jnp.int32, (peers * slots, rows), 0).astype(F32)
+    pack = (peer * slots + rank == slot).astype(BF16)
+    incoming = lax.broadcasted_iota(jnp.int32, (rows, peers * slots), 1)
+    origin = lax.shift_right_logical(incoming, log2(slots)).astype(F32)
+    within = (incoming & (slots - 1))[:1].astype(F32)
+    amount = jnp.sum(jnp.where(sender == origin, 1.0, 0.0), axis=0, keepdims=True)
+    base = jnp.sum(jnp.where(sender < origin, 1.0, 0.0), axis=0, keepdims=True)
+    wanted = jnp.where(within < amount, base + within, -1.0)
+    place = lax.broadcasted_iota(jnp.int32, (rows, peers * slots), 0).astype(F32)
+    return pack, (wanted == place).astype(BF16), row_place
+
+
 def exchange_kernel(
-    peers, row_count, x_hbm, row_slot_ref, row_place_ref, slot_row_ref, send_slot_ref,
+    peers, row_count, slots, x_hbm, ids_ref, send_slot_ref,
     own_hbm, other_hbm, both_hbm, early_hbm, tri_ref, note_ref,
     x_buf, out_buf, in_buf, both_buf, other_buf, early_buf, gram_buf, cross_buf, place_out, place_in, note_out, note_in,
     tri_buf, parts, total,
@@ -55,7 +85,6 @@
     me = col % peers
     mirror = lax.rem(col + peers, 2 * peers)
     half = CHUNKS // 2
-    slots = out_buf.shape[2]
     width = out_buf.shape[3]
     rows = other_buf.shape[1]
 
@@ -88,8 +117,7 @@
         pl.semaphore_signal(barrier, inc=1, device_id=ring_device(step), device_id_type=MESH)
     pl.semaphore_wait(barrier, peers - 1 + count - 1)
 
-    slot = lax.broadcasted_iota(jnp.int32, (peers * slots, rows), 0)
-    pack = (row_slot_ref[...] == slot).astype(BF16)
+    pack, compact, row_place = slot_tables(ids_ref[...], col, peers, slots)
 
     def send_chunk(index, carry):
         read_chunk(index).wait()
@@ -111,9 +139,54 @@
         in_buf[index, me] = out_buf[index, me]
         return carry
 
-    lax.fori_loop(0, CHUNKS, send_chunk, 0)
-
-    places = jnp.broadcast_to(row_place_ref[...].astype(F32), (128, rows)).T
+    def arrived(index):
+        pltpu.make_async_copy(
+            in_buf.at[index, pl.ds(0, peers - 1)], in_buf.at[index, pl.ds(0, peers - 1)], in_sem.at[index]
+        ).wait()
+        return select_rows(compact, in_buf[index].reshape(peers * slots, width))
+
+    def cross_copy(index):
+        return pltpu.make_async_remote_copy(
+            src_ref=other_buf.at[index],
+            dst_ref=both_buf.at[index, pl.ds(pl.multiple_of(side * rows, rows), rows)],
+            send_sem=z_out_sem.at[index],
+            recv_sem=z_in_sem.at[index],
+            device_id={"col": mirror},
+            device_id_type=MESH,
+        )
+
+    def write_other(index):
+        return pltpu.make_async_copy(other_buf.at[index], other_hbm.at[index], write_sem.at[index])
+
+    def write_own(index):
+        source = both_buf.at[EARLY + index, pl.ds(pl.multiple_of(side * rows, rows), rows)]
+        return pltpu.make_async_copy(source, own_hbm.at[index], write_sem.at[half + index])
+
+    def write_both(index):
+        return pltpu.make_async_copy(both_buf.at[index], both_hbm.at[index], write_sem.at[2 * half + index])
+
+    def cross_chunk(index, carry):
+        other_buf[index] = arrived(index)
+        cross_copy(index).start()
+        write_other(index).start()
+        return carry
+
+    def keep_chunk(index, carry):
+        both_buf[index, pl.ds(pl.multiple_of(side * rows, rows), rows)] = arrived(half + index)
+        return carry
+
+    def send_and_cross(index, carry):
+        send_chunk(index + LEAD, carry)
+        return cross_chunk(index, carry)
+
+    def send_and_keep(index, carry):
+        send_chunk(half + index + LEAD, carry)
+        return keep_chunk(index, carry)
+
+    lax.fori_loop(0, LEAD, send_chunk, 0)
+    lax.fori_loop(0, half, send_and_cross, 0)
+    lax.fori_loop(0, half - LEAD, send_and_keep, 0)
+    places = jnp.broadcast_to(row_place, (128, rows)).T
     place_out[...] = select_rows(pack, places).reshape(peers, slots, 128)
 
     def send_places(step, carry):
@@ -131,48 +204,7 @@
     lax.fori_loop(1, peers, send_places, 0)
     place_in[me] = place_out[me]
 
-    place = lax.broadcasted_iota(jnp.int32, (rows, peers * slots), 0)
-    compact = (slot_row_ref[...] == place).astype(BF16)
-
-    def arrived(index):
-        pltpu.make_async_copy(
-            in_buf.at[index, pl.ds(0, peers - 1)], in_buf.at[index, pl.ds(0, peers - 1)], in_sem.at[index]
-        ).wait()
-        return select_rows(compact, in_buf[index].reshape(peers * slots, width))
-
-    def cross_copy(index):
-        return pltpu.make_async_remote_copy(
-            src_ref=other_buf.at[index],
-            dst_ref=both_buf.at[index, pl.ds(pl.multiple_of(side * rows, rows), rows)],
-            send_sem=z_out_sem.at[index],
-            recv_sem=z_in_sem.at[index],
-            device_id={"col": mirror},
-            device_id_type=MESH,
-        )
-
-    def write_other(index):
-        return pltpu.make_async_copy(other_buf.at[index], other_hbm.at[index], write_sem.at[index])
-
-    def write_own(index):
-        source = both_buf.at[EARLY + index, pl.ds(pl.multiple_of(side * rows, rows), rows)]
-        return pltpu.make_async_copy(source, own_hbm.at[index], write_sem.at[half + index])
-
-    def write_both(index):
-        return pltpu.make_async_copy(both_buf.at[index], both_hbm.at[index], write_sem.at[2 * half + index])
-
-    def cross_chunk(index, carry):
-        other_buf[index] = arrived(index)
-        cross_copy(index).start()
-        write_other(index).start()
-        return carry
-
-    lax.fori_loop(0, half, cross_chunk, 0)
-
-    def keep_chunk(index, carry):
-        both_buf[index, pl.ds(pl.multiple_of(side * rows, rows), rows)] = arrived(half + index)
-        return carry
-
-    lax.fori_loop(0, half, keep_chunk, 0)
+    lax.fori_loop(half - LEAD, half, keep_chunk, 0)
     for index in range(half - EARLY):
         write_own(index).start()
 
@@ -220,11 +252,21 @@
     quarter = rows // 2
     place = 0
     for i in range(4):
-        for j in range(i + 1):
-            tri_buf[place * quarter:(place + 1) * quarter, :] = gram[
-                i * quarter:(i + 1) * quarter, j * quarter:(j + 1) * quarter
-            ]
-            place += 1
+        for j in range(i):
+            tri_buf[place:place + quarter, :] = gram[i * quarter:(i + 1) * quarter, j * quarter:(j + 1) * quarter]
+            place += quarter
+    eighth = quarter // 2
+    for i in range(4):
+        low = i * quarter + eighth
+        tri_buf[place:place + eighth, :] = gram[low:low + eighth, i * quarter:(i + 1) * quarter]
+        place += eighth
+    for i in (0, 2):
+        first, second = i * quarter, (i + 1) * quarter
+        tri_buf[place:place + eighth, :] = jnp.concatenate(
+            [gram[first:first + eighth, first:first + eighth], gram[second:second + eighth, second:second + eighth]],
+            axis=1,
+        )
+        place += eighth
 
     size = parts.shape[1]
 
@@ -251,7 +293,8 @@
             device_id_type=MESH,
         )
 
-    for step in range(1, count):
+    far_first = sorted(range(1, count), key=lambda step: -min(step, count - step))
+    for step in far_first:
         part_copy(step).start()
     early_copy(1).start()
     parts[ring] = tri_buf[piece(ring), :]
@@ -261,7 +304,7 @@
     for index in range(1, count):
         value = value + parts[index]
     total[ring] = value
-    for step in range(1, count):
+    for step in far_first:
         total_copy(step).start()
     pltpu.make_async_copy(pieces, pieces, sum_sem.at[3]).wait()
     tri_ref[...] = total[...].reshape(tri_ref.shape)
@@ -301,26 +344,25 @@
     lax.fori_loop(0, CHUNKS, sent, 0)
 
 
-def exchange(x, row_slot, row_place, slot_row, send_slot, peers, row_count):
+def exchange(x, dest_ids, send_slot, peers, slots, row_count):
     rows, columns = x.shape
     width = columns // CHUNKS
     half = CHUNKS // 2
     count = 2 * row_count
-    slots = slot_row.shape[1] // peers
     any_space = pl.BlockSpec(memory_space=pl.ANY)
     vmem = pl.BlockSpec(memory_space=pltpu.VMEM)
     smem = pl.BlockSpec(memory_space=pltpu.SMEM)
     return pl.pallas_call(
-        functools.partial(exchange_kernel, peers, row_count),
+        functools.partial(exchange_kernel, peers, row_count, slots),
         out_shape=[
             jax.ShapeDtypeStruct((half - EARLY, rows, width), F32),
             jax.ShapeDtypeStruct((half, rows, width), F32),
             jax.ShapeDtypeStruct((half, 2 * rows, width), F32),
             jax.ShapeDtypeStruct((EARLY, rows, width), F32),
-            jax.ShapeDtypeStruct((10 * rows // 2, rows // 2), F32),
+            jax.ShapeDtypeStruct((9 * rows // 2, rows // 2), F32),
             jax.ShapeDtypeStruct((2, 8, rows), F32),
         ],
-        in_specs=[any_space, vmem, vmem, vmem, smem],
+        in_specs=[any_space, vmem, smem],
         out_specs=[any_space, any_space, any_space, any_space, vmem, vmem],
         scratch_shapes=[
             pltpu.VMEM((CHUNKS, rows, width), F32),
@@ -335,9 +377,9 @@
             pltpu.VMEM((peers, slots, 128), F32),
             pltpu.VMEM((8, rows), F32),
             pltpu.VMEM((2, 8, rows), F32),
-            pltpu.VMEM((10 * rows // 2, rows // 2), F32),
-            pltpu.VMEM((count, 5 * rows // count, rows // 2), F32),
-            pltpu.VMEM((count, 5 * rows // count, rows // 2), F32),
+            pltpu.VMEM((9 * rows // 2, rows // 2), F32),
+            pltpu.VMEM((count, 9 * rows // 2 // count, rows // 2), F32),
+            pltpu.VMEM((count, 9 * rows // 2 // count, rows // 2), F32),
             pltpu.SemaphoreType.DMA((CHUNKS,)),
             pltpu.SemaphoreType.DMA((CHUNKS,)),
             pltpu.SemaphoreType.DMA((CHUNKS,)),
@@ -354,7 +396,7 @@
         ),
         cost_estimate=pl.CostEstimate(flops=10**10, bytes_accessed=10**8, transcendentals=0),
         name="exchange",
-    )(x, row_slot, row_place, slot_row, send_slot)
+    )(x, dest_ids[None, :], send_slot)
 
 
 def inverse_factors(blocks):
@@ -448,12 +490,21 @@
     size = 2 * quarter
     place = 0
     for i in range(4):
-        for j in range(i + 1):
-            block = tri_ref[place * quarter:(place + 1) * quarter, :]
+        for j in range(i):
+            block = tri_ref[place:place + quarter, :]
             gram_buf[i * quarter:(i + 1) * quarter, j * quarter:(j + 1) * quarter] = block
-            if i != j:
-                gram_buf[j * quarter:(j + 1) * quarter, i * quarter:(i + 1) * quarter] = block.T
-            place += 1
+            gram_buf[j * quarter:(j + 1) * quarter, i * quarter:(i + 1) * quarter] = block.T
+            place += quarter
+    eighth = quarter // 2
+    corners = place + 4 * eighth
+    for i in range(4):
+        lower = tri_ref[place:place + eighth, :]
+        row = corners + i // 2 * eighth
+        corner = tri_ref[row:row + eighth, i % 2 * eighth:(i % 2 + 1) * eighth]
+        upper = jnp.concatenate([corner, lower[:, :eighth].T], axis=1)
+        span = slice(i * quarter, (i + 1) * quarter)
+        gram_buf[span, span] = jnp.concatenate([upper, lower], axis=0)
+        place += eighth
     side = side_ref[0]
     position = jnp.concatenate([note_ref[0, :1], note_ref[1, :1]], axis=1)
     slot = lax.broadcasted_iota(jnp.int32, (2 * size, 2 * size), 0)
@@ -587,29 +638,6 @@
     )(side, high, low, high, low, own, early, mirror, partial)
 
 
-def slot_tables(dest_ids, col, peers, slots):
-    rows = dest_ids.shape[0]
-    count = 2 * peers
-    local = jnp.arange(rows, dtype=jnp.int32)
-    target = dest_ids // rows
-    peer = target % peers
-    earlier = (peer[:, None] == peer[None, :]) & (local[None, :] < local[:, None])
-    rank = jnp.sum(earlier.astype(jnp.int32), axis=1)
-    row_slot = peer * slots + rank
-    row_place = target // peers * rows + dest_ids % rows
-    offset = (target - col) % peers
-    amount = jnp.sum((offset[None, :] == jnp.arange(peers, dtype=jnp.int32)[:, None]).astype(jnp.int32), axis=1)
-    sender = jnp.arange(peers, dtype=jnp.int32)
-    sender_offset = (col - sender) % peers
-    from_sender = jnp.sum(
-        jnp.where(sender_offset[:, None] == jnp.arange(peers, dtype=jnp.int32)[None, :], amount[None, :], 0), axis=1
-    )
-    base = jnp.sum(jnp.where(sender[None, :] < sender[:, None], from_sender[None, :], 0), axis=1)
-    within = jnp.arange(slots, dtype=jnp.int32)
-    slot_row = jnp.where(within[None, :] < from_sender[:, None], base[:, None] + within[None, :], -1).reshape(-1)
-    return row_slot[None, :], row_place[None, :], slot_row[None, :]
-
-
 def body(row_count, greens_matrix, dest_ids, send_slot):
     rows, columns = greens_matrix.shape
     count = lax.axis_size("col")
@@ -618,9 +646,8 @@
     slots = 2 * cap
     col = lax.axis_index("col")
     side = (col // peers).astype(jnp.int32)[None]
-    row_slot, row_place, slot_row = slot_tables(dest_ids, col, peers, slots)
     own, other, both, early, tri, note = exchange(
-        greens_matrix, row_slot, row_place, slot_row, send_slot, peers, row_count
+        greens_matrix, dest_ids, send_slot, peers, slots, row_count
     )
     mirror = lax.ppermute(own, "col", [(i, i ^ peers) for i in range(count)])
     high, low = rotations(tri, note, side)

time: 261 us -> 251 us (0.962)
  Pallas kernels: 235 us -> 229 us
  other arithmetic: 3.23 us -> 0 us
    pallas_call x1, Pallas kernels: 174 us -> 168 us  [exchange(): pl.pallas_call(functools.partial(exchange_kernel, peers, row_count, slots...]
  transfers between devices with their start and end apart: 1 -> 1, of which waited for: 1 -> 1; matrix products, arithmetic and copies ran while one was open for 0% -> 0% of each run, Pallas kernels for 22% -> 23%
where the time goes in v4:
time: 251 us; the launch traced here: 246 us
  Pallas kernels  229 us (91%)
  waiting for transfers between devices  11.3 us (5%)
  starting transfers between devices  3.34 us (1%)
    pallas_call x1, Pallas kernels, exchange(): pl.pallas_call(functools.partial(exchange_kernel, peers, row_count, slots...  168 us
    pallas_call x1, Pallas kernels, rotations(): pl.pallas_call(rotation_kernel, out_shape=[jax.ShapeDtypeStruct((size, 2...  54 us
    ppermute x1, waiting for transfers between devices, body(): mirror = lax.ppermute(own, 'col', [(i, i ^ peers) for i in range(count)])  11.3 us
  transfers between devices with their start and end apart: 1, of which 1 were waited for; matrix products, arithmetic and copies ran while one was open for 0% of the time, Pallas kernels for 23%

profile of v4, /device:TPU:1, one launch (start us, length us, event | category | flops | bytes accessed | tf_op | source)
XLA Modules:
  0.0 246.0 jit_solution(5082802035118533827)
XLA Ops:
  0.7 167.7 %exchange.1 = (f32[6,256,256]{2,1,0:T(8,128)}, f32[8,256,256]{2,1,0:T(8,128)}, f32[8,512,256]{2,1,0:T(8,128)}, f32[2,256,256]{2,1,0:T(8,128)}, f32[1152,128]{1,0:T(8,128)}, /*index=5*/f32[2,8,256]{2,1,0:T(8,128)}) custom-call(f32[256,4096]{1,0:T(8,128)} %x_hbm.1, s32[1,256]{1,0:T(1,128)} %bitcast.2, s32[1]{0:T(128)S(6)} %copy.6.send_slot_ref), custom_call_target="tpu_custom_call" | custom-call | flops 10000000000 | bytes 100000000 | tf_op jit(solution)/shard_map/exchange/pallas_call | solution.py:355
  168.4 3.3 %collective-permute-start = (f32[6,256,256]{2,1,0:T(8,128)}, f32[6,256,256]{2,1,0:T(8,128)S(1)}, u32[]{:S(2)}, u32[]{:S(2)}) collective-permute-start(f32[6,256,256]{2,1,0:T(8,128)} %get-tuple-element.19), channel_id=1, source_target_pairs={{0,128},{4,132},{8,136},{12,140},{16,144},{20,148},{24,152},{28,15... | collective-permute-start | bytes 4718600 | tf_op jit(solution)/shard_map/ppermute | solution.py:652
  171.7 0.0 copy-start.3
  171.7 1.1 copy-done.3
  172.8 0.0 copy-start.4
  172.8 0.7 copy-done.4
  173.5 0.0 copy-start
  173.5 54.0 %rotations.1 = (bf16[256,512]{1,0:T(8,128)(2,1)S(1)}, bf16[256,512]{1,0:T(8,128)(2,1)S(1)}) custom-call(f32[1152,128]{1,0:T(8,128)S(1)} %copy-done.3, f32[2,8,256]{2,1,0:T(8,128)S(1)} %copy-done.4, s32[1]{0:T(128)} %bitcast.side_ref), custom_call_target="tpu_custom_call" | custom-call | flops 60000002048 | bytes 100000000 | tf_op jit(solution)/shard_map/rotations/pallas_call | solution.py:547
  227.5 0.0 copy-done
  227.5 0.0 copy-start.1
  227.6 0.0 copy-start.2
  227.6 3.5 %apply_both.1.partial_ref = f32[256,4096]{1,0:T(8,128)} custom-call(s32[1]{0:T(128)} %bitcast.side_ref, bf16[256,512]{1,0:T(8,128)(2,1)S(1)} %get-tuple-element.15.high_ref.mirror_high_ref, bf16[256,512]{1,0:T(8,128)(2,1)S(1)} %get-tuple-element.16.low_ref.mirror_low_ref, f32[8,512,256]{2,1,0:T(8,128)S(1)} %copy-done), custom_call_target="tpu_custom_call" | custom-call | flops 10000000000 | bytes 10000000 | tf_op jit(solution)/shard_map/apply_both/pallas_call | solution.py:581
  231.0 11.3 %collective-permute-done.mirror_ref = f32[6,256,256]{2,1,0:T(8,128)S(1)} collective-permute-done((f32[6,256,256]{2,1,0:T(8,128)}, f32[6,256,256]{2,1,0:T(8,128)S(1)}, u32[]{:S(2)}, u32[]{:S(2)}) %collective-permute-start) | collective-permute-done | bytes 1572896 | tf_op jit(solution)/shard_map/ppermute | solution.py:652
  242.4 0.0 copy-done.1
  242.4 0.0 copy-done.2
  242.4 3.5 %apply_rest.1 = f32[256,4096]{1,0:T(8,128)} custom-call(s32[1]{0:T(128)} %bitcast.side_ref, bf16[256,512]{1,0:T(8,128)(2,1)S(1)} %get-tuple-element.15.high_ref.mirror_high_ref, bf16[256,512]{1,0:T(8,128)(2,1)S(1)} %get-tuple-element.16.low_ref.mirror_low_ref, ...), custom_call_target="tpu_custom_call", output_to_operand_aliasing={{}: (8, {})} | custom-call | flops 10000000000 | bytes 10000000 | tf_op jit(solution)/shard_map/apply_rest/pallas_call | solution.py:616
Async XLA Ops:
  168.4 74.0 %collective-permute-start = (f32[6,256,256]{2,1,0:T(8,128)}, f32[6,256,256]{2,1,0:T(8,128)S(1)}, u32[]{:S(2)}, u32[]{:S(2)}) collective-permute-start(f32[6,256,256]{2,1,0:T(8,128)} %get-tuple-element.19), channel_id=1, source_target_pairs={{0,128},{4,132},{8,136},{12,140},{16,144},{20,148},{24,152},{28,15... | collective-permute-start | bytes 4718600 | tf_op jit(solution)/shard_map/ppermute | solution.py:652
  171.7 1.1 copy-start.3
  172.8 0.7 copy-start.4
  173.5 54.1 %copy-start = (f32[8,512,256]{2,1,0:T(8,128)S(1)}, f32[8,512,256]{2,1,0:T(8,128)}, u32[]{:S(2)}) copy-start(f32[8,512,256]{2,1,0:T(8,128)} %get-tuple-element.20.both_ref) | copy-start | bytes 12582916
  227.5 14.8 %copy-start.1 = (f32[8,256,256]{2,1,0:T(8,128)S(1)}, f32[8,256,256]{2,1,0:T(8,128)}, u32[]{:S(2)}) copy-start(f32[8,256,256]{2,1,0:T(8,128)} %get-tuple-element.17.own_ref) | copy-start | bytes 6291460
  227.6 14.8 %copy-start.2 = (f32[2,256,256]{2,1,0:T(8,128)S(1)}, f32[2,256,256]{2,1,0:T(8,128)}, u32[]{:S(2)}) copy-start(f32[2,256,256]{2,1,0:T(8,128)} %get-tuple-element.18.early_ref) | copy-start | bytes 1572868

commit v5 on v4

--- a/solution.py
+++ b/solution.py
@@ -176,8 +176,8 @@
         return carry
 
     def send_and_cross(index, carry):
-        send_chunk(index + LEAD, carry)
-        return cross_chunk(index, carry)
+        cross_chunk(index, carry)
+        return send_chunk(index + LEAD, carry)
 
     def send_and_keep(index, carry):
         send_chunk(half + index + LEAD, carry)

time: 251 us -> 251 us (level)
  no operation moved by 1% of the time
where the time goes in v5:
time: 251 us; the launch traced here: 246 us
  Pallas kernels  229 us (91%)
  waiting for transfers between devices  11.3 us (5%)
  starting transfers between devices  3.34 us (1%)
    pallas_call x1, Pallas kernels, exchange(): pl.pallas_call(functools.partial(exchange_kernel, peers, row_count, slots...  168 us
    pallas_call x1, Pallas kernels, rotations(): pl.pallas_call(rotation_kernel, out_shape=[jax.ShapeDtypeStruct((size, 2...  54 us
    ppermute x1, waiting for transfers between devices, body(): mirror = lax.ppermute(own, 'col', [(i, i ^ peers) for i in range(count)])  11.3 us
  transfers between devices with their start and end apart: 1, of which 1 were waited for; matrix products, arithmetic and copies ran while one was open for 0% of the time, Pallas kernels for 23%

profile of v5, /device:TPU:1, one launch (start us, length us, event | category | flops | bytes accessed | tf_op | source)
XLA Modules:
  0.0 246.1 jit_solution(3005746476883308063)
XLA Ops:
  0.7 167.7 %exchange.1 = (f32[6,256,256]{2,1,0:T(8,128)}, f32[8,256,256]{2,1,0:T(8,128)}, f32[8,512,256]{2,1,0:T(8,128)}, f32[2,256,256]{2,1,0:T(8,128)}, f32[1152,128]{1,0:T(8,128)}, /*index=5*/f32[2,8,256]{2,1,0:T(8,128)}) custom-call(f32[256,4096]{1,0:T(8,128)} %x_hbm.1, s32[1,256]{1,0:T(1,128)} %bitcast.2, s32[1]{0:T(128)S(6)} %copy.6.send_slot_ref), custom_call_target="tpu_custom_call" | custom-call | flops 10000000000 | bytes 100000000 | tf_op jit(solution)/shard_map/exchange/pallas_call | solution.py:355
  168.4 3.3 %collective-permute-start = (f32[6,256,256]{2,1,0:T(8,128)}, f32[6,256,256]{2,1,0:T(8,128)S(1)}, u32[]{:S(2)}, u32[]{:S(2)}) collective-permute-start(f32[6,256,256]{2,1,0:T(8,128)} %get-tuple-element.19), channel_id=1, source_target_pairs={{0,128},{4,132},{8,136},{12,140},{16,144},{20,148},{24,152},{28,15... | collective-permute-start | bytes 4718600 | tf_op jit(solution)/shard_map/ppermute | solution.py:652
  171.7 0.0 copy-start.3
  171.7 1.1 copy-done.3
  172.8 0.0 copy-start.4
  172.8 0.7 copy-done.4
  173.5 0.0 copy-start
  173.5 54.0 %rotations.1 = (bf16[256,512]{1,0:T(8,128)(2,1)S(1)}, bf16[256,512]{1,0:T(8,128)(2,1)S(1)}) custom-call(f32[1152,128]{1,0:T(8,128)S(1)} %copy-done.3, f32[2,8,256]{2,1,0:T(8,128)S(1)} %copy-done.4, s32[1]{0:T(128)} %bitcast.side_ref), custom_call_target="tpu_custom_call" | custom-call | flops 60000002048 | bytes 100000000 | tf_op jit(solution)/shard_map/rotations/pallas_call | solution.py:547
  227.5 0.0 copy-done
  227.5 0.0 copy-start.1
  227.6 0.0 copy-start.2
  227.6 3.5 %apply_both.1.partial_ref = f32[256,4096]{1,0:T(8,128)} custom-call(s32[1]{0:T(128)} %bitcast.side_ref, bf16[256,512]{1,0:T(8,128)(2,1)S(1)} %get-tuple-element.15.high_ref.mirror_high_ref, bf16[256,512]{1,0:T(8,128)(2,1)S(1)} %get-tuple-element.16.low_ref.mirror_low_ref, f32[8,512,256]{2,1,0:T(8,128)S(1)} %copy-done), custom_call_target="tpu_custom_call" | custom-call | flops 10000000000 | bytes 10000000 | tf_op jit(solution)/shard_map/apply_both/pallas_call | solution.py:581
  231.0 11.3 %collective-permute-done.mirror_ref = f32[6,256,256]{2,1,0:T(8,128)S(1)} collective-permute-done((f32[6,256,256]{2,1,0:T(8,128)}, f32[6,256,256]{2,1,0:T(8,128)S(1)}, u32[]{:S(2)}, u32[]{:S(2)}) %collective-permute-start) | collective-permute-done | bytes 1572896 | tf_op jit(solution)/shard_map/ppermute | solution.py:652
  242.3 0.0 copy-done.1
  242.4 0.0 copy-done.2
  242.4 3.5 %apply_rest.1 = f32[256,4096]{1,0:T(8,128)} custom-call(s32[1]{0:T(128)} %bitcast.side_ref, bf16[256,512]{1,0:T(8,128)(2,1)S(1)} %get-tuple-element.15.high_ref.mirror_high_ref, bf16[256,512]{1,0:T(8,128)(2,1)S(1)} %get-tuple-element.16.low_ref.mirror_low_ref, ...), custom_call_target="tpu_custom_call", output_to_operand_aliasing={{}: (8, {})} | custom-call | flops 10000000000 | bytes 10000000 | tf_op jit(solution)/shard_map/apply_rest/pallas_call | solution.py:616
Async XLA Ops:
  168.4 74.0 %collective-permute-start = (f32[6,256,256]{2,1,0:T(8,128)}, f32[6,256,256]{2,1,0:T(8,128)S(1)}, u32[]{:S(2)}, u32[]{:S(2)}) collective-permute-start(f32[6,256,256]{2,1,0:T(8,128)} %get-tuple-element.19), channel_id=1, source_target_pairs={{0,128},{4,132},{8,136},{12,140},{16,144},{20,148},{24,152},{28,15... | collective-permute-start | bytes 4718600 | tf_op jit(solution)/shard_map/ppermute | solution.py:652
  171.7 1.1 copy-start.3
  172.8 0.7 copy-start.4
  173.5 54.1 %copy-start = (f32[8,512,256]{2,1,0:T(8,128)S(1)}, f32[8,512,256]{2,1,0:T(8,128)}, u32[]{:S(2)}) copy-start(f32[8,512,256]{2,1,0:T(8,128)} %get-tuple-element.20.both_ref) | copy-start | bytes 12582916
  227.5 14.8 %copy-start.1 = (f32[8,256,256]{2,1,0:T(8,128)S(1)}, f32[8,256,256]{2,1,0:T(8,128)}, u32[]{:S(2)}) copy-start(f32[8,256,256]{2,1,0:T(8,128)} %get-tuple-element.17.own_ref) | copy-start | bytes 6291460
  227.6 14.8 %copy-start.2 = (f32[2,256,256]{2,1,0:T(8,128)S(1)}, f32[2,256,256]{2,1,0:T(8,128)}, u32[]{:S(2)}) copy-start(f32[2,256,256]{2,1,0:T(8,128)} %get-tuple-element.18.early_ref) | copy-start | bytes 1572868
